TPU v7x, 32 devices: a whole 2x2x4 slice. The times are simulated.
32 devices in a mesh: parts: 2 (over y), slab: 4 (over z), valley: 2 (over x), blk: 2 (over core).
Axes of the slice: x: 2, y: 2, z: 4, core: 2. Of those that a mesh axis runs over, the one named last changes fastest.
Arguments:
- potential: bfloat16 [64, 2048], P('slab'), may hold values from -3.5 to 4
- mode_density: bfloat16 [4, 2048, 2048], P(('parts', 'valley'), 'blk'), parts along dimension 0, may hold values from 0 to 1, as said below
- energy: float32 [4], P(('parts', 'valley')), parts along dimension 0, may hold values from -0.5 to 0.5
- hopping: float32 [4], P(('parts', 'valley')), parts along dimension 0, may hold values from 0.6 to 1.4
- mode_energy: float32 [4, 2048], P(('parts', 'valley'), 'blk'), parts along dimension 0, may hold values from -2.5 to 3
- broadening: float32 [4, 2048], P(('parts', 'valley'), 'blk'), parts along dimension 0, may hold values from 0.0078125 to 0.3
- self_left: float32 [4, 2, 2048], P(('parts', 'valley'), None, 'blk'), parts along dimension 0, may hold values from -1 to 1, as said below
- self_right: float32 [4, 2, 2048], P(('parts', 'valley'), None, 'blk'), parts along dimension 0, may hold values from -1 to 1, as said below
- occupation: float32 [4], P(('parts', 'valley')), parts along dimension 0, may hold values from 0.5 to 1.5
Outputs:
- mode_charge: float32 [4, 64, 2048], P(('parts', 'valley'), 'slab', 'blk'), parts along dimension 0
- electron_density: float32 [128, 2048], P(('parts', 'slab'), ('valley', 'blk')), parts along dimension 0
There are 2 independent parts, one for each index of `parts`. A program takes and returns all parts, laid end to end along the dimension named above; an argument that names none is the same for every part. Nothing has to cross between parts.
Inputs may be any that keep to these rules, and one draw needn't show every extreme that they name: `mode_density`: every entry is positive. `self_left`: the imaginary parts (index 1 of the second dimension) are negative. `self_right`: the imaginary parts (index 1 of the second dimension) are negative.
All inputs are finite; a program needn't handle non-finite values.
Results may differ from a plain program's by a relative error of at most 0.0065.
Values sent between devices are 32-bit elements; how exact they have to be, the bound alone decides.
No kernel may reach another device: no remote copies, remote signals or barrier semaphores. Data moves between devices by JAX's collectives and lax.ppermute only.
A program may use at most 64 MiB of HBM per device.

v0:
```python
import math

import jax
import jax.numpy as jnp
from jax import lax
from jax.sharding import PartitionSpec as P


def complex_times(first_re, first_im, second_re, second_im):
    return (
        first_re * second_re - first_im * second_im,
        first_re * second_im + first_im * second_re,
    )


def complex_divide(first_re, first_im, second_re, second_im):
    magnitude = second_re * second_re + second_im * second_im
    return (
        (first_re * second_re + first_im * second_im) / magnitude,
        (first_im * second_re - first_re * second_im) / magnitude,
    )


def compose(second_map, first_map):
    entries = []
    for row_pos in range(2):
        for col_pos in range(2):
            first_slot = 4 * row_pos
            second_slot = 2 * col_pos
            head_re, head_im = complex_times(
                second_map[first_slot],
                second_map[first_slot + 1],
                first_map[second_slot],
                first_map[second_slot + 1],
            )
            tail_re, tail_im = complex_times(
                second_map[first_slot + 2],
                second_map[first_slot + 3],
                first_map[second_slot + 4],
                first_map[second_slot + 5],
            )
            entries.append(head_re + tail_re)
            entries.append(head_im + tail_im)
    stacked = jnp.stack(entries)
    largest = jnp.max(jnp.abs(stacked), axis=0)
    return stacked / largest


def combine_maps(earlier, following):
    return compose(following, earlier)


def build_maps(onsite_re, onsite_im, hop_square):
    blank = jnp.zeros_like(onsite_re)
    return jnp.stack(
        [blank, blank, blank + 1.0, blank, blank - hop_square, blank, onsite_re, onsite_im]
    )


def mobius(mapping, value_re, value_im):
    upper_re, upper_im = complex_times(mapping[0], mapping[1], value_re, value_im)
    lower_re, lower_im = complex_times(mapping[4], mapping[5], value_re, value_im)
    return complex_divide(
        upper_re + mapping[2], upper_im + mapping[3], lower_re + mapping[6], lower_im + mapping[7]
    )


def charge_from(
    onsite_re,
    onsite_im,
    hop_square,
    forward,
    backward,
    left_re,
    left_im,
    right_re,
    right_im,
    occupied,
    axis_pos,
):
    conn_left_re, conn_left_im = mobius(forward, left_re, left_im)
    conn_right_re, conn_right_im = mobius(backward, right_re, right_im)
    length = onsite_re.shape[axis_pos]
    prior_re = jnp.concatenate(
        [
            left_re + 0.0 * lax.slice_in_dim(onsite_re, 0, 1, axis=axis_pos),
            lax.slice_in_dim(conn_left_re, 0, length - 1, axis=axis_pos),
        ],
        axis=axis_pos,
    )
    prior_im = jnp.concatenate(
        [
            left_im + 0.0 * lax.slice_in_dim(onsite_re, 0, 1, axis=axis_pos),
            lax.slice_in_dim(conn_left_im, 0, length - 1, axis=axis_pos),
        ],
        axis=axis_pos,
    )
    later_re = jnp.concatenate(
        [
            lax.slice_in_dim(conn_right_re, 1, length, axis=axis_pos),
            right_re + 0.0 * lax.slice_in_dim(onsite_re, 0, 1, axis=axis_pos),
        ],
        axis=axis_pos,
    )
    later_im = jnp.concatenate(
        [
            lax.slice_in_dim(conn_right_im, 1, length, axis=axis_pos),
            right_im + 0.0 * lax.slice_in_dim(onsite_re, 0, 1, axis=axis_pos),
        ],
        axis=axis_pos,
    )
    bottom_re = onsite_re - hop_square * (prior_re + later_re)
    bottom_im = onsite_im - hop_square * (prior_im + later_im)
    return occupied / math.pi * bottom_im / (bottom_re * bottom_re + bottom_im * bottom_im)


def select_modes(values, offset, count):
    return lax.dynamic_slice_in_dim(values, offset, count, 0)


def body(
    potential,
    mode_density,
    energy,
    hopping,
    mode_energy,
    broadening,
    self_left,
    self_right,
    occupation,
):
    profile_rows = mode_density[0]
    projected = lax.dot_general(
        potential, profile_rows, (((1,), (1,)), ((), ())), preferred_element_type=jnp.float32
    )
    slab_count, half_width = projected.shape
    hop_square = hopping[0] * hopping[0]
    occupied = occupation[0]
    groups = lax.axis_size("slab")
    width_piece = half_width // groups
    gathered = lax.all_to_all(
        projected.reshape(slab_count, groups, width_piece),
        "slab",
        split_axis=1,
        concat_axis=0,
        tiled=True,
    )
    chain_pot = gathered[:, 0, :].T
    offset = lax.axis_index("slab") * width_piece
    mode_piece = select_modes(mode_energy[0], offset, width_piece)
    broad_piece = select_modes(broadening[0], offset, width_piece)
    onsite_re = energy[0] - mode_piece[:, None] - chain_pot
    onsite_im = jnp.broadcast_to(broad_piece[:, None], chain_pot.shape)
    mapping = build_maps(onsite_re, onsite_im, hop_square)
    forward = lax.associative_scan(combine_maps, mapping, axis=2)
    backward = lax.associative_scan(combine_maps, mapping, reverse=True, axis=2)
    left_re = select_modes(self_left[0, 0], offset, width_piece)[:, None] / hop_square
    left_im = select_modes(self_left[0, 1], offset, width_piece)[:, None] / hop_square
    right_re = select_modes(self_right[0, 0], offset, width_piece)[:, None] / hop_square
    right_im = select_modes(self_right[0, 1], offset, width_piece)[:, None] / hop_square
    chain_charge = charge_from(
        onsite_re,
        onsite_im,
        hop_square,
        forward,
        backward,
        left_re,
        left_im,
        right_re,
        right_im,
        occupied,
        1,
    )
    returned = lax.all_to_all(
        chain_charge.T.reshape(slab_count * groups, 1, width_piece),
        "slab",
        split_axis=0,
        concat_axis=1,
        tiled=True,
    )
    charge = returned.reshape(slab_count, half_width)
    partial_terms = jnp.dot(
        charge.astype(jnp.bfloat16), profile_rows, preferred_element_type=jnp.float32
    )
    density = lax.psum_scatter(partial_terms, ("valley", "blk"), scatter_dimension=1, tiled=True)
    return (charge[None], density)


def solution(mesh):
    placed = (
        P("slab", None),
        P(("parts", "valley"), "blk", None),
        P(("parts", "valley")),
        P(("parts", "valley")),
        P(("parts", "valley"), "blk"),
        P(("parts", "valley"), "blk"),
        P(("parts", "valley"), None, "blk"),
        P(("parts", "valley"), None, "blk"),
        P(("parts", "valley")),
    )
    return jax.shard_map(
        body,
        mesh=mesh,
        in_specs=placed,
        out_specs=(P(("parts", "valley"), "slab", "blk"), P(("parts", "slab"), ("valley", "blk"))),
        check_vma=False,
    )
```

profile of v0, /device:TPU:0, one launch (start us, length us, event | category | flops | bytes accessed | tf_op | source)
XLA Modules:
  0.0 73.4 jit_solution(14656460760758439376)
XLA Ops:
  7.2 0.8 %copy-done = bf16[16,2048]{1,0:T(8,128)(2,1)S(1)} copy-done((bf16[16,2048]{1,0:T(8,128)(2,1)S(1)}, bf16[16,2048]{1,0:T(8,128)(2,1)}, u32[]{:S(2)}) %copy-start) | copy-done | bytes 65560
  8.0 4.0 %fusion.17 = f32[16,4,256]{2,0,1:T(8,128)} fusion(bf16[4,256,2048]{2,1,0:T(8,128)(2,1)} %bitcast.159, bf16[16,2048]{1,0:T(8,128)(2,1)S(1)} %copy-done), kind=kOutput, calls=%fused_computation.248 | convolution fusion | flops 67108864 | bytes 4325376 | tf_op jit(solution)/shard_map/dot_general | solution.py:133
  12.0 6.3 %all-to-all-start = ((f32[16,4,256]{2,0,1:T(8,128)}), f32[16,4,256]{2,0,1:T(8,128)S(1)}, u32[]{:S(2)}, u32[]{:S(2)}) async-start(f32[16,4,256]{2,0,1:T(8,128)} %fusion.17), calls=%async_computation | async-start | bytes 131072 | tf_op jit(solution)/shard_map/all_to_all | solution.py:141
  20.4 0.7 constant_dynamic-slice_fusion.5
  21.1 3.0 %all-to-all-done = f32[16,4,256]{2,0,1:T(8,128)S(1)} async-done(((f32[16,4,256]{2,0,1:T(8,128)}), f32[16,4,256]{2,0,1:T(8,128)S(1)}, u32[]{:S(2)}, u32[]{:S(2)}) %all-to-all-start) | async-done | bytes 65568 | tf_op jit(solution)/shard_map/all_to_all | solution.py:141
  24.1 0.1 slice.1825
  24.3 0.1 slice.1827
  24.5 0.1 slice.2032
  24.6 0.1 slice.2034
  24.7 0.1 slice.2036
  24.7 0.1 slice.2038
  24.8 0.1 slice.2033
  24.9 0.1 slice.2035
  25.0 0.1 slice.2039
  25.2 0.1 slice.2041
  25.3 0.1 slice.2042
  25.4 0.1 slice.2043
  25.5 0.1 slice.2045
  25.6 0.1 slice.2044
  25.7 0.1 slice.2046
  25.7 0.1 slice.2047
  26.0 0.1 slice.2051
  26.1 0.1 slice.2053
  27.5 0.1 slice.2049
  27.6 0.1 slice.2029
  28.0 0.1 slice.1846
  28.1 0.1 slice.1848
  29.6 0.1 slice.1844
  29.7 0.2 slice.1823
  30.1 0.1 pad.76
  30.2 0.1 pad.77
  31.0 0.1 pad.81
  31.1 0.1 pad.83
  31.5 0.1 pad.82
  31.9 0.2 pad.524
  32.1 0.2 pad.525
  32.6 0.1 pad.88
  32.8 0.1 pad.89
  33.5 0.1 pad.93
  33.7 0.1 pad.95
  34.0 0.1 pad.94
  34.1 0.1 slice.2031
  34.2 0.1 slice.2210
  34.3 0.1 slice.2213
  34.4 0.1 slice.2216
  34.6 0.1 slice.2223
  34.7 0.1 slice.2225
  34.8 0.1 slice.2227
  34.9 0.1 slice.2229
  35.3 0.2 pad.526
  35.4 0.2 pad.527
  35.6 0.1 slice_add_fusion.4
  35.7 0.1 slice.2247
  35.8 0.1 slice.2231
  35.8 0.1 slice.2234
  35.9 0.1 slice.2237
  36.0 0.1 slice.2239
  36.1 0.1 slice.2241
  36.1 0.1 slice.2243
  36.2 0.1 slice.2245
  36.6 8.1 %all_to_all.30 = f32[64,1,256]{2,1,0:T(1,128)S(1)} all-to-all(f32[64,1,256]{2,1,0:T(1,128)S(1)} %reshape.1755), channel_id=1, replica_groups=mesh['parts'=2,'slab'=4,'valley'=2,'blk'=2] {'slab'}, dimensions={0} | all-to-all | bytes 131072 | tf_op jit(solution)/shard_map/all_to_all | solution.py:174
  44.8 3.5 %fusion = f32[16,2048]{1,0:T(8,128)} fusion(bf16[16,1024]{1,0:T(8,128)(2,1)S(1)} %bitcast.206, bf16[1,1024,2048]{2,1,0:T(8,128)(2,1)} %param.10), kind=kOutput, calls=%fused_computation | convolution fusion | flops 67108864 | bytes 4358144 | tf_op jit(solution)/shard_map/dot_general | solution.py:182
  48.3 0.7 broadcast_in_dim_reshape.3
  49.0 17.6 %reduce-scatter.2.cloned.1.call-done = f32[16,512]{1,0:T(8,128)} async-done(((f32[16,2048]{1,0:T(8,128)}), f32[16,512]{1,0:T(8,128)}) %reduce-scatter.2.cloned.1.call-update) | async-done | bytes 32784 | tf_op jit(solution)/shard_map/reduce_scatter | solution.py:185
  (310 shorter events, 5.7 us)
Async XLA Ops:
  7.2 0.8 %copy-start = (bf16[16,2048]{1,0:T(8,128)(2,1)S(1)}, bf16[16,2048]{1,0:T(8,128)(2,1)}, u32[]{:S(2)}) copy-start(bf16[16,2048]{1,0:T(8,128)(2,1)} %param.9) | copy-start | bytes 196612
  7.2 13.2 %copy-start.3 = (f32[1,2,1024]{2,1,0:T(2,128)S(1)}, f32[1,2,1024]{2,1,0:T(2,128)}, u32[]{:S(2)}) copy-start(f32[1,2,1024]{2,1,0:T(2,128)} %param.15) | copy-start | bytes 24580
  7.2 13.2 %copy-start.2 = (f32[1,2,1024]{2,1,0:T(2,128)S(1)}, f32[1,2,1024]{2,1,0:T(2,128)}, u32[]{:S(2)}) copy-start(f32[1,2,1024]{2,1,0:T(2,128)} %param.16) | copy-start | bytes 24580
  12.0 12.1 %all-to-all-start = ((f32[16,4,256]{2,0,1:T(8,128)}), f32[16,4,256]{2,0,1:T(8,128)S(1)}, u32[]{:S(2)}, u32[]{:S(2)}) async-start(f32[16,4,256]{2,0,1:T(8,128)} %fusion.17), calls=%async_computation | async-start | bytes 131072 | tf_op jit(solution)/shard_map/all_to_all | solution.py:141
  18.3 48.2 %reduce-scatter.2.cloned.1.call-start = ((), (), s32[]{:S(2)}) async-start(), calls=%async_computation.3 | async-start | bytes 163840 | tf_op jit(solution)/shard_map/reduce_scatter | solution.py:185
  26.6 2.3 %copy-start.1 = (f32[8,256,8]{1,2,0:T(8,128)}, f32[8,256,8]{1,2,0:T(8,128)S(1)}, u32[]{:S(2)}) copy-start(f32[8,256,8]{1,2,0:T(8,128)S(1)} %broadcast_divide_fusion.9) | copy-start | bytes 196612
  31.6 1.6 %slice-start = ((f32[8,256,8]{1,2,0:T(8,128)}), f32[8,256,1]{1,2,0:T(1,128)S(1)}, s32[]{:S(2)}) async-start(f32[8,256,8]{1,2,0:T(8,128)} %copy-done.1), calls=%async_computation.4 | async-start | bytes 16384 | tf_op jit(solution)/shard_map/slice | solution.py:156
Sparse Core Ops, SparseCore 0:
  48.4 18.1 reduce-scatter.1
where the time goes:
time: 73.8 us; the launch traced here: 73.4 us
  waiting for transfers between devices  20.6 us (28%)
  between operations  18 us (24%)
  blocking collectives  8.11 us (11%)
  local copies, waits for them, and re-layouts  7.8 us (11%)
  matrix products  7.5 us (10%)
  starting transfers between devices  6.32 us (9%)
  other arithmetic  5.12 us (7%)
    reduce_scatter x1, waiting for transfers between devices, body(): lax.psum_scatter(partial_terms, ('valley', 'blk'), scatter_dimension=1, t...  17.6 us
    all_to_all x1, blocking collectives, body(): lax.all_to_all(chain_charge.T.reshape(slab_count * groups, 1, width_piece...  8.11 us
    all_to_all x1, starting transfers between devices, body(): lax.all_to_all(projected.reshape(slab_count, groups, width_piece), 'slab'...  6.32 us
    dot_general x1, matrix products, body(): lax.dot_general(potential, profile_rows, (((1,), (1,)), ((), ())), prefer...  4.01 us
    dot_general x1, matrix products, body(): jnp.dot(charge.astype(jnp.bfloat16), profile_rows, preferred_element_type...  3.49 us
    all_to_all x1, waiting for transfers between devices, body(): lax.all_to_all(projected.reshape(slab_count, groups, width_piece), 'slab'...  2.97 us
    unnamed x153, other arithmetic  2.46 us
    unnamed x22, local copies, waits for them, and re-layouts  1.5 us
  transfers between devices with their start and end apart: 2, of which 2 were waited for; matrix products, arithmetic and copies ran while one was open for 2% of the time, Pallas kernels for 0%

commit v1 on v0

v1 whole, which is shorter than its diff:
```python
import math

import jax
import jax.numpy as jnp
from jax import lax
from jax.experimental import pallas as pl
from jax.experimental.pallas import tpu as pltpu
from jax.sharding import PartitionSpec as P

LANES = 128
VMEM_LIMIT = 24 * 1024 * 1024


def times(first, second):
    return (
        first[0] * second[0] - first[1] * second[1],
        first[0] * second[1] + first[1] * second[0],
    )


def plus(first, second):
    return first[0] + second[0], first[1] + second[1]


def minus(first, second):
    return first[0] - second[0], first[1] - second[1]


def invert(value):
    scale = 1.0 / (value[0] * value[0] + value[1] * value[1])
    return value[0] * scale, -(value[1] * scale)


def one_minus(value):
    return 1.0 - value[0], -value[1]


def extend(run, slab):
    low, high, through = run
    grown = invert(minus(slab, high))
    return (
        plus(low, times(through, grown)),
        grown,
        times(through, times(grown, grown)),
    )


def join(first, second):
    low1, high1, through1 = first
    low2, high2, through2 = second
    bridge = invert(one_minus(times(high1, low2)))
    return (
        plus(low1, times(times(through1, low2), bridge)),
        plus(high2, times(times(through2, high1), bridge)),
        times(times(through1, through2), times(bridge, bridge)),
    )


def flip(run):
    return run[1], run[0], run[2]


def carry(run, value):
    low, high, through = run
    return plus(high, times(times(through, value), invert(one_minus(times(low, value)))))


def pick(flag, chosen, otherwise):
    return jax.tree.map(lambda a, b: jnp.where(flag, a, b), chosen, otherwise)


def pack(run):
    return jnp.stack([part for pair in run for part in pair])


def unpack(stack):
    return tuple((stack[2 * k], stack[2 * k + 1]) for k in range(stack.shape[0] // 2))


def fold_row(row, fold):
    for group in range(fold.shape[0]):
        fold[group : group + 1, :] = row[:, group * LANES : (group + 1) * LANES]
    return fold[...]


def project_kernel(
    energy,
    hopping,
    potential,
    mode_energy,
    broadening,
    self_left,
    self_right,
    profile_hbm,
    onsite_out,
    contact_out,
    run_out,
    profile,
    staged,
    fold,
    arrived,
):
    slabs = potential.shape[0]
    groups = profile.shape[0] // LANES
    copies = []
    for group in range(groups):
        rows = pl.ds(group * LANES, LANES)
        copies.append(
            pltpu.make_async_copy(profile_hbm.at[0, rows], profile.at[rows], arrived.at[group])
        )
        copies[-1].start()
    inverse = 1.0 / jnp.full((groups, LANES), hopping[0], jnp.float32)
    level = (energy[0] - fold_row(mode_energy, fold.at[0])) * inverse
    damping = fold_row(broadening, fold.at[1]) * inverse
    for part in range(2):
        contact_out[part] = fold_row(self_left.at[0, part : part + 1], fold.at[2 + part]) * inverse
        contact_out[2 + part] = (
            fold_row(self_right.at[0, part : part + 1], fold.at[4 + part]) * inverse
        )
    for group in range(groups):
        copies[group].wait()
        staged[group * slabs : (group + 1) * slabs, :] = lax.dot_general(
            potential[...],
            profile[group * LANES : (group + 1) * LANES, :],
            (((1,), (1,)), ((), ())),
            preferred_element_type=jnp.float32,
        )
    runs = []
    length = math.gcd(slabs, 4)
    onsite_out[slabs] = damping
    for start in range(0, slabs, length):
        run = None
        for slab in range(start, start + length):
            real = level - staged[pl.ds(slab, groups, stride=slabs), :] * inverse
            onsite_out[slab] = real
            onsite = (real, damping)
            if run is None:
                alone = invert(onsite)
                run = (alone, alone, times(alone, alone))
            else:
                run = extend(run, onsite)
        runs.append(run)
    while len(runs) > 1:
        paired = [join(runs[k], runs[k + 1]) for k in range(0, len(runs) - 1, 2)]
        runs = paired + runs[2 * len(paired) :]
    for place, part in enumerate(part for pair in runs[0] for part in pair):
        run_out[place] = part


def charge_kernel(
    hopping,
    occupation,
    upper,
    onsite_in,
    outer_in,
    inner_run,
    sent_in,
    profile,
    charge_out,
    density_out,
    staged,
):
    slabs = onsite_in.shape[0] - 1
    groups = onsite_in.shape[1]
    outer = (outer_in[0], outer_in[1])
    inner = carry(
        tuple((inner_run[2 * k], inner_run[2 * k + 1]) for k in range(3)), (sent_in[0], sent_in[1])
    )
    is_upper = upper[0] > 0
    left = pick(is_upper, inner, outer)
    right = pick(is_upper, outer, inner)
    damping = onsite_in[slabs]
    weight = jnp.full((groups, LANES), occupation[0], jnp.float32) / (
        jnp.full((groups, LANES), hopping[0], jnp.float32) * math.pi
    )
    lefts, rights = [left], [right]
    for slab in range(slabs - 1):
        lefts.append(invert(minus((onsite_in[slab], damping), lefts[-1])))
        rights.append(invert(minus((onsite_in[slabs - 1 - slab], damping), rights[-1])))
    for slab in range(slabs):
        below = minus((onsite_in[slab], damping), plus(lefts[slab], rights[slabs - 1 - slab]))
        staged[pl.ds(slab, groups, stride=slabs), :] = (
            weight * below[1] / (below[0] * below[0] + below[1] * below[1])
        )
    for group in range(groups):
        charge_out[0, :, group * LANES : (group + 1) * LANES] = staged[
            group * slabs : (group + 1) * slabs, :
        ]
    half = charge_out[0].astype(jnp.bfloat16)
    width = density_out.shape[1]
    step = math.gcd(width, 256)
    for start in range(0, width, step):
        density_out[:, start : start + step] = jnp.dot(
            half, profile[0, :, start : start + step], preferred_element_type=jnp.float32
        )


def body(
    potential,
    mode_density,
    energy,
    hopping,
    mode_energy,
    broadening,
    self_left,
    self_right,
    occupation,
):
    slabs, width = potential.shape
    modes = mode_density.shape[1]
    groups = modes // LANES
    smem = pl.BlockSpec(memory_space=pltpu.SMEM)
    vmem = pl.BlockSpec(memory_space=pltpu.VMEM)
    anywhere = pl.BlockSpec(memory_space=pl.ANY)
    f32 = jnp.float32
    onsite, contact, run = pl.pallas_call(
        project_kernel,
        out_shape=(
            jax.ShapeDtypeStruct((slabs + 1, groups, LANES), f32),
            jax.ShapeDtypeStruct((4, groups, LANES), f32),
            jax.ShapeDtypeStruct((6, groups, LANES), f32),
        ),
        in_specs=[smem, smem, vmem, vmem, vmem, vmem, vmem, anywhere],
        out_specs=(vmem, vmem, vmem),
        scratch_shapes=[
            pltpu.VMEM((modes, width), jnp.bfloat16),
            pltpu.VMEM((groups * slabs, LANES), f32),
            pltpu.VMEM((6, groups, LANES), f32),
            pltpu.SemaphoreType.DMA((groups,)),
        ],
        compiler_params=pltpu.CompilerParams(vmem_limit_bytes=VMEM_LIMIT),
        cost_estimate=pl.CostEstimate(
            flops=2 * slabs * width * modes, bytes_accessed=2 * width * modes, transcendentals=0
        ),
    )(energy, hopping, potential, mode_energy, broadening, self_left, self_right, mode_density)

    count = lax.axis_size("slab")
    place = lax.axis_index("slab")
    group = unpack(run)
    zero = jnp.zeros((groups, LANES), f32)
    nothing = ((zero, zero), (zero, zero), (zero + 1.0, zero))
    before, after = nothing, nothing
    left_end, right_end = unpack(contact)
    reach = 1
    while 2 * reach < count:
        pairs = [(k, k ^ reach) for k in range(count)]
        other = unpack(lax.ppermute(pack(group), "slab", pairs))
        is_second = (place & reach) > 0
        if reach == 1:
            before, after = pick(is_second, other, nothing), pick(is_second, nothing, other)
        else:
            before, after = (
                pick(is_second, join(other, before), before),
                pick(is_second, after, join(after, other)),
            )
        group = join(pick(is_second, other, group), pick(is_second, group, other))
        reach *= 2
    is_upper = (place & reach) > 0
    end = pick(is_upper, right_end, left_end)
    if count > 1:
        sent = pack((carry(pick(is_upper, flip(group), group), end),))
        sent = lax.ppermute(sent, "slab", [(k, k ^ reach) for k in range(count)])
    else:
        sent = pack((right_end,))
    outer = pack((carry(pick(is_upper, flip(after), before), end),))
    inner_run = pack(pick(is_upper, before, flip(after)))
    upper = is_upper.astype(jnp.int32).reshape(1)

    charge, density = pl.pallas_call(
        charge_kernel,
        out_shape=(
            jax.ShapeDtypeStruct((1, slabs, modes), f32),
            jax.ShapeDtypeStruct((slabs, width), f32),
        ),
        in_specs=[smem, smem, smem, vmem, vmem, vmem, vmem, vmem],
        out_specs=(vmem, vmem),
        scratch_shapes=[pltpu.VMEM((groups * slabs, LANES), f32)],
        compiler_params=pltpu.CompilerParams(vmem_limit_bytes=VMEM_LIMIT),
        cost_estimate=pl.CostEstimate(
            flops=2 * slabs * width * modes, bytes_accessed=2 * width * modes, transcendentals=0
        ),
    )(hopping, occupation, upper, onsite, outer, inner_run, sent, mode_density)

    valleys, blocks = lax.axis_size("valley"), lax.axis_size("blk")
    piece = width // (valleys * blocks)
    terms = density.reshape(slabs, valleys, blocks, piece)
    for name, axis in (("blk", 2), ("valley", 1)):
        number, index = lax.axis_size(name), lax.axis_index(name)
        total = lax.dynamic_index_in_dim(terms, index, axis, keepdims=True)
        for shift in range(1, number):
            away = lax.dynamic_index_in_dim(terms, (index + shift) % number, axis, keepdims=True)
            total = total + lax.ppermute(
                away, name, [(k, (k + shift) % number) for k in range(number)]
            )
        terms = total
    return charge, terms.reshape(slabs, piece)


def solution(mesh):
    placed = (
        P("slab", None),
        P(("parts", "valley"), "blk", None),
        P(("parts", "valley")),
        P(("parts", "valley")),
        P(("parts", "valley"), "blk"),
        P(("parts", "valley"), "blk"),
        P(("parts", "valley"), None, "blk"),
        P(("parts", "valley"), None, "blk"),
        P(("parts", "valley")),
    )
    return jax.shard_map(
        body,
        mesh=mesh,
        in_specs=placed,
        out_specs=(P(("parts", "valley"), "slab", "blk"), P(("parts", "slab"), ("valley", "blk"))),
        check_vma=False,
    )
```

time: 73.8 us -> 31.3 us (0.42)
  between operations: 18 us -> 2.71 us
  waiting for transfers between devices: 20.6 us -> 6.07 us
  blocking collectives: 8.11 us -> 0 us
  matrix products: 7.5 us -> 0 us
  Pallas kernels: 0 us -> 4.94 us
  other arithmetic: 5.12 us -> 0.77 us
  starting transfers between devices: 6.32 us -> 8.14 us
    reduce_scatter x1 -> x0, waiting for transfers between devices: 17.6 us -> none  [body(): lax.psum_scatter(partial_terms, ('valley', 'blk'), scatter_dimension=1, t...]
    ppermute x0 -> x4, starting transfers between devices: none -> 8.14 us  [the longest x1 3.1 us: body(): sent = lax.ppermute(sent, 'slab', [(k, k ^ reach) for k in range(count)])]
    all_to_all x1 -> x0, blocking collectives: 8.11 us -> none  [body(): lax.all_to_all(chain_charge.T.reshape(slab_count * groups, 1, width_piece...]
    dot_general x2 -> x0, matrix products: 7.5 us -> none  [the longest x1 4.01 us: body(): lax.dot_general(potential, profile_rows, (((1,), (1,)), ((), ())), prefer...]
    unnamed x22 -> x15, local copies, waits for them, and re-layouts: 1.5 us -> 7.99 us
    all_to_all x1 -> x0, starting transfers between devices: 6.32 us -> none  [body(): lax.all_to_all(projected.reshape(slab_count, groups, width_piece), 'slab'...]
    ppermute x0 -> x4, waiting for transfers between devices: none -> 6.07 us  [the longest x2 3.32 us: body(): lax.ppermute(away, name, [(k, (k + shift) % number) for k in range(number)])]
    pallas_call x0 -> x2, Pallas kernels: none -> 4.94 us  [the longest x1 3.61 us: body(): pl.pallas_call(project_kernel, out_shape=(jax.ShapeDtypeStruct((slabs + 1...]
  transfers between devices with their start and end apart: 2 -> 4, of which waited for: 2 -> 4; matrix products, arithmetic and copies ran while one was open for 2% -> 0% of each run, Pallas kernels for 0% -> 0%
where the time goes in v1:
time: 31.3 us; the launch traced here: 30.9 us
  local copies, waits for them, and re-layouts  8.23 us (26%)
  starting transfers between devices  8.14 us (26%)
  waiting for transfers between devices  6.07 us (19%)
  Pallas kernels  4.94 us (16%)
  between operations  2.71 us (9%)
  other arithmetic  0.77 us (2%)
    unnamed x15, local copies, waits for them, and re-layouts  7.99 us
    pallas_call x1, Pallas kernels, body(): pl.pallas_call(project_kernel, out_shape=(jax.ShapeDtypeStruct((slabs + 1...  3.61 us
    ppermute x2, waiting for transfers between devices, body(): lax.ppermute(away, name, [(k, (k + shift) % number) for k in range(number)])  3.32 us
    ppermute x1, starting transfers between devices, body(): sent = lax.ppermute(sent, 'slab', [(k, k ^ reach) for k in range(count)])  3.1 us
    ppermute x1, starting transfers between devices, body(): other = unpack(lax.ppermute(pack(group), 'slab', pairs))  3.09 us
    ppermute x2, starting transfers between devices, body(): lax.ppermute(away, name, [(k, (k + shift) % number) for k in range(number)])  1.96 us
    ppermute x1, waiting for transfers between devices, body(): sent = lax.ppermute(sent, 'slab', [(k, k ^ reach) for k in range(count)])  1.61 us
    pallas_call x1, Pallas kernels, body(): pl.pallas_call(charge_kernel, out_shape=(jax.ShapeDtypeStruct((1, slabs,...  1.34 us
  transfers between devices with their start and end apart: 4, of which 4 were waited for; matrix products, arithmetic and copies ran while one was open for 0% of the time, Pallas kernels for 0%

profile of v1, /device:TPU:0, one launch (start us, length us, event | category | flops | bytes accessed | tf_op | source)
XLA Modules:
  0.0 30.9 jit_solution(1180175060092207554)
XLA Ops:
  1.9 0.0 copy-start
  1.9 2.2 %copy-done = bf16[1,1024,2048]{2,1,0:T(8,128)(2,1)S(1)} copy-done((bf16[1,1024,2048]{2,1,0:T(8,128)(2,1)S(1)}, bf16[1,1024,2048]{2,1,0:T(8,128)(2,1)}, u32[]{:S(2)}) %copy-start) | copy-done | bytes 4194328
  4.1 0.0 copy-start.2
  4.1 0.8 %copy-done.2 = bf16[16,2048]{1,0:T(8,128)(2,1)S(1)} copy-done((bf16[16,2048]{1,0:T(8,128)(2,1)S(1)}, bf16[16,2048]{1,0:T(8,128)(2,1)}, u32[]{:S(2)}) %copy-start.2) | copy-done | bytes 65560
  5.0 0.0 copy-start.3
  5.0 0.7 %copy-done.3 = f32[1,2,1024]{2,1,0:T(2,128)S(1)} copy-done((f32[1,2,1024]{2,1,0:T(2,128)S(1)}, f32[1,2,1024]{2,1,0:T(2,128)}, u32[]{:S(2)}) %copy-start.3) | copy-done | bytes 8216
  5.7 0.0 copy-start.4
  5.7 0.7 %copy-done.4 = f32[1,2,1024]{2,1,0:T(2,128)S(1)} copy-done((f32[1,2,1024]{2,1,0:T(2,128)S(1)}, f32[1,2,1024]{2,1,0:T(2,128)}, u32[]{:S(2)}) %copy-start.4) | copy-done | bytes 8216
  6.3 0.0 copy-start.5
  6.4 0.7 %copy-done.5 = f32[1,1024]{1,0:T(1,128)S(1)} copy-done((f32[1,1024]{1,0:T(1,128)S(1)}, f32[1,1024]{1,0:T(1,128)}, u32[]{:S(2)}) %copy-start.5) | copy-done | bytes 4120
  7.0 0.0 copy-start.6
  7.0 0.7 %copy-done.6 = f32[1,1024]{1,0:T(1,128)S(1)} copy-done((f32[1,1024]{1,0:T(1,128)S(1)}, f32[1,1024]{1,0:T(1,128)}, u32[]{:S(2)}) %copy-start.6) | copy-done | bytes 4120
  7.7 3.6 %shard_map.104 = (f32[17,8,128]{2,1,0:T(8,128)S(1)}, f32[4,8,128]{2,1,0:T(8,128)S(1)}, f32[6,8,128]{2,1,0:T(8,128)S(1)}) custom-call(f32[1]{0:T(128)S(6)} %copy.21.energy, f32[1]{0:T(128)S(6)} %copy.22.hopping, bf16[16,2048]{1,0:T(8,128)(2,1)S(1)} %copy-done.2, f32[1,1024]{1,0:T(1,128)S(1)} %copy-done.5, f32[1,1024]{1,0:T(1,128)S(1)} %copy-done.6, ...), custom_call_target="tpu_custom_call" | custom-call | flops 67108864 | bytes 4194304 | tf_op jit(solution)/shard_map/pallas_call | solution.py:216
  11.3 3.1 %collective-permute-start = (f32[6,8,128]{2,1,0:T(8,128)S(1)}, f32[6,8,128]{2,1,0:T(8,128)S(1)}, u32[]{:S(2)}, u32[]{:S(2)}) collective-permute-start(f32[6,8,128]{2,1,0:T(8,128)S(1)} %get-tuple-element.8), channel_id=1, source_target_pairs={{0,4},{4,0},{8,12},{12,8},{1,5},{5,1},{9,13},{13,9},{2,6},{6,2},{1... | collective-permute-start | bytes 73736 | tf_op jit(solution)/shard_map/ppermute | solution.py:247
  15.1 1.1 %collective-permute-done = f32[6,8,128]{2,1,0:T(8,128)S(1)} collective-permute-done((f32[6,8,128]{2,1,0:T(8,128)S(1)}, f32[6,8,128]{2,1,0:T(8,128)S(1)}, u32[]{:S(2)}, u32[]{:S(2)}) %collective-permute-start) | collective-permute-done | bytes 24608 | tf_op jit(solution)/shard_map/ppermute | solution.py:247
  16.4 3.1 %collective-permute-start.1 = (f32[2,8,128]{2,1,0:T(8,128)S(1)}, f32[2,8,128]{2,1,0:T(8,128)S(1)}, u32[]{:S(2)}, u32[]{:S(2)}) collective-permute-start(f32[2,8,128]{2,1,0:T(8,128)S(1)} %pad_maximum_fusion.1), channel_id=1, source_target_pairs={{0,8},{4,12},{8,0},{12,4},{1,9},{5,13},{9,1},{13,5},{2,10},{6,14},... | collective-permute-start | bytes 24584 | tf_op jit(solution)/shard_map/ppermute | solution.py:262
  19.5 1.6 %collective-permute-done.1.sent_in = f32[2,8,128]{2,1,0:T(8,128)S(1)} collective-permute-done((f32[2,8,128]{2,1,0:T(8,128)S(1)}, f32[2,8,128]{2,1,0:T(8,128)S(1)}, u32[]{:S(2)}, u32[]{:S(2)}) %collective-permute-start.1) | collective-permute-done | bytes 8224 | tf_op jit(solution)/shard_map/ppermute | solution.py:262
  21.1 0.0 copy-start.1
  21.1 2.2 %copy-done.1 = bf16[1,1024,2048]{2,1,0:T(8,128)(2,1)S(1)} copy-done((bf16[1,1024,2048]{2,1,0:T(8,128)(2,1)S(1)}, bf16[1,1024,2048]{2,1,0:T(8,128)(2,1)}, u32[]{:S(2)}) %copy-start.1) | copy-done | bytes 4194328
  23.3 1.3 %shard_map.105 = (f32[1,16,1024]{2,1,0:T(8,128)}, f32[16,2048]{1,0:T(8,128)S(1)}) custom-call(f32[1]{0:T(128)S(6)} %copy.22.hopping, f32[1]{0:T(128)S(6)} %copy.23.occupation, s32[1]{0:T(128)} %bitcast.upper, f32[17,8,128]{2,1,0:T(8,128)S(1)} %get-tuple-element.7.onsite_in, f32[2,8,128]{2,1,0:T(8,128)S(1)} %pad_maximum_fusion.outer_in, ...), custom_call_target="tpu_custom_call" | custom-call | flops 67108864 | bytes 4194304 | tf_op jit(solution)/shard_map/pallas_call | solution.py:269
  24.6 0.1 reshape.17
  24.8 0.1 constant_dynamic-slice_fusion.2
  24.9 0.1 collective-permute-start.2
  25.0 1.2 %collective-permute-done.2 = f32[16,2,1,512]{3,0,2,1:T(8,128)S(1)} collective-permute-done((f32[16,2,1,512]{3,0,2,1:T(8,128)S(1)}, f32[16,2,1,512]{3,0,2,1:T(8,128)S(1)}, u32[]{:S(2)}, u32[]{:S(2)}) %collective-permute-start.2) | collective-permute-done | bytes 65568 | tf_op jit(solution)/shard_map/ppermute | solution.py:292
  26.3 1.9 %collective-permute-start.3 = (f32[16,1,1,512]{3,0,2,1:T(8,128)S(1)}, f32[16,1,1,512]{3,0,2,1:T(8,128)S(1)}, u32[]{:S(2)}, u32[]{:S(2)}) collective-permute-start(f32[16,1,1,512]{3,0,2,1:T(8,128)S(1)} %constant_dynamic-slice_fusion), channel_id=1, source_target_pairs={{0,2},{2,0},{1,3},{3,1},{4,6},{6,4},{5,7},{7,5},{8,10},{10,8},{9,1... | collective-permute-start | bytes 98312 | tf_op jit(solution)/shard_map/ppermute | solution.py:292
  28.2 2.1 %collective-permute-done.3 = f32[16,1,1,512]{3,0,2,1:T(8,128)S(1)} collective-permute-done((f32[16,1,1,512]{3,0,2,1:T(8,128)S(1)}, f32[16,1,1,512]{3,0,2,1:T(8,128)S(1)}, u32[]{:S(2)}, u32[]{:S(2)}) %collective-permute-start.3) | collective-permute-done | bytes 32800 | tf_op jit(solution)/shard_map/ppermute | solution.py:292
  30.2 0.6 %add_bitcast_fusion = f32[16,512]{1,0:T(8,128)} fusion(f32[16,1,1,512]{3,0,2,1:T(8,128)S(1)} %collective-permute-done.3, f32[16,2,1,512]{3,0,2,1:T(8,128)S(1)} %copy_add_fusion, s32[]{:T(128)S(6)} %select_n.336), kind=kLoop, calls=%fused_computation.1 | loop fusion | flops 8192 | bytes 98308 | tf_op jit(solution)/shard_map/reshape | solution.py:296
  (13 shorter events, 0.2 us)
Async XLA Ops:
  1.9 2.2 %copy-start = (bf16[1,1024,2048]{2,1,0:T(8,128)(2,1)S(1)}, bf16[1,1024,2048]{2,1,0:T(8,128)(2,1)}, u32[]{:S(2)}) copy-start(bf16[1,1024,2048]{2,1,0:T(8,128)(2,1)} %profile.1) | copy-start | bytes 12582916
  4.1 0.8 %copy-start.2 = (bf16[16,2048]{1,0:T(8,128)(2,1)S(1)}, bf16[16,2048]{1,0:T(8,128)(2,1)}, u32[]{:S(2)}) copy-start(bf16[16,2048]{1,0:T(8,128)(2,1)} %potential.1) | copy-start | bytes 196612
  5.0 0.7 %copy-start.3 = (f32[1,2,1024]{2,1,0:T(2,128)S(1)}, f32[1,2,1024]{2,1,0:T(2,128)}, u32[]{:S(2)}) copy-start(f32[1,2,1024]{2,1,0:T(2,128)} %self_left.1) | copy-start | bytes 24580
  5.7 0.7 %copy-start.4 = (f32[1,2,1024]{2,1,0:T(2,128)S(1)}, f32[1,2,1024]{2,1,0:T(2,128)}, u32[]{:S(2)}) copy-start(f32[1,2,1024]{2,1,0:T(2,128)} %self_right.1) | copy-start | bytes 24580
  6.3 0.7 %copy-start.5 = (f32[1,1024]{1,0:T(1,128)S(1)}, f32[1,1024]{1,0:T(1,128)}, u32[]{:S(2)}) copy-start(f32[1,1024]{1,0:T(1,128)} %mode_energy.1) | copy-start | bytes 12292
  7.0 0.7 %copy-start.6 = (f32[1,1024]{1,0:T(1,128)S(1)}, f32[1,1024]{1,0:T(1,128)}, u32[]{:S(2)}) copy-start(f32[1,1024]{1,0:T(1,128)} %broadening.1) | copy-start | bytes 12292
  11.3 4.9 %collective-permute-start = (f32[6,8,128]{2,1,0:T(8,128)S(1)}, f32[6,8,128]{2,1,0:T(8,128)S(1)}, u32[]{:S(2)}, u32[]{:S(2)}) collective-permute-start(f32[6,8,128]{2,1,0:T(8,128)S(1)} %get-tuple-element.8), channel_id=1, source_target_pairs={{0,4},{4,0},{8,12},{12,8},{1,5},{5,1},{9,13},{13,9},{2,6},{6,2},{1... | collective-permute-start | bytes 73736 | tf_op jit(solution)/shard_map/ppermute | solution.py:247
  16.4 4.7 %collective-permute-start.1 = (f32[2,8,128]{2,1,0:T(8,128)S(1)}, f32[2,8,128]{2,1,0:T(8,128)S(1)}, u32[]{:S(2)}, u32[]{:S(2)}) collective-permute-start(f32[2,8,128]{2,1,0:T(8,128)S(1)} %pad_maximum_fusion.1), channel_id=1, source_target_pairs={{0,8},{4,12},{8,0},{12,4},{1,9},{5,13},{9,1},{13,5},{2,10},{6,14},... | collective-permute-start | bytes 24584 | tf_op jit(solution)/shard_map/ppermute | solution.py:262
  21.1 2.2 %copy-start.1 = (bf16[1,1024,2048]{2,1,0:T(8,128)(2,1)S(1)}, bf16[1,1024,2048]{2,1,0:T(8,128)(2,1)}, u32[]{:S(2)}) copy-start(bf16[1,1024,2048]{2,1,0:T(8,128)(2,1)} %profile.1) | copy-start | bytes 12582916
  24.9 1.3 %collective-permute-start.2 = (f32[16,2,1,512]{3,0,2,1:T(8,128)S(1)}, f32[16,2,1,512]{3,0,2,1:T(8,128)S(1)}, u32[]{:S(2)}, u32[]{:S(2)}) collective-permute-start(f32[16,2,1,512]{3,0,2,1:T(8,128)S(1)} %copy.14), channel_id=1, source_target_pairs={{0,1},{1,0},{2,3},{3,2},{4,5},{5,4},{6,7},{7,6},{8,9},{9,8},{10,11... | collective-permute-start | bytes 196616 | tf_op jit(solution)/shard_map/ppermute | solution.py:292
  26.3 4.0 %collective-permute-start.3 = (f32[16,1,1,512]{3,0,2,1:T(8,128)S(1)}, f32[16,1,1,512]{3,0,2,1:T(8,128)S(1)}, u32[]{:S(2)}, u32[]{:S(2)}) collective-permute-start(f32[16,1,1,512]{3,0,2,1:T(8,128)S(1)} %constant_dynamic-slice_fusion), channel_id=1, source_target_pairs={{0,2},{2,0},{1,3},{3,1},{4,6},{6,4},{5,7},{7,5},{8,10},{10,8},{9,1... | collective-permute-start | bytes 98312 | tf_op jit(solution)/shard_map/ppermute | solution.py:292

commit v2 on v1

v2 whole, which is shorter than its diff:
```python
import functools
import math

import jax
import jax.numpy as jnp
from jax import lax
from jax.experimental import pallas as pl
from jax.experimental.pallas import tpu as pltpu
from jax.sharding import PartitionSpec as P

LANES = 128
VMEM_LIMIT = 24 * 1024 * 1024
SMALL_LIMIT = 8 * 1024 * 1024


def times(first, second):
    return (
        first[0] * second[0] - first[1] * second[1],
        first[0] * second[1] + first[1] * second[0],
    )


def plus(first, second):
    return first[0] + second[0], first[1] + second[1]


def minus(first, second):
    return first[0] - second[0], first[1] - second[1]


def invert(value):
    scale = 1.0 / (value[0] * value[0] + value[1] * value[1])
    return value[0] * scale, -(value[1] * scale)


def one_minus(value):
    return 1.0 - value[0], -value[1]


def extend(run, slab):
    low, high, through = run
    grown = invert(minus(slab, high))
    return (
        plus(low, times(through, grown)),
        grown,
        times(through, times(grown, grown)),
    )


def join(first, second):
    low1, high1, through1 = first
    low2, high2, through2 = second
    bridge = invert(one_minus(times(high1, low2)))
    return (
        plus(low1, times(times(through1, low2), bridge)),
        plus(high2, times(times(through2, high1), bridge)),
        times(times(through1, through2), times(bridge, bridge)),
    )


def flip(run):
    return run[1], run[0], run[2]


def carry(run, value):
    low, high, through = run
    return plus(high, times(times(through, value), invert(one_minus(times(low, value)))))


def pick(flag, chosen, otherwise):
    return jax.tree.map(lambda a, b: jnp.where(flag, a, b), chosen, otherwise)


def pack(run):
    return jnp.stack([part for pair in run for part in pair])


def unpack(stack):
    return tuple((stack[2 * k], stack[2 * k + 1]) for k in range(stack.shape[0] // 2))


def fold_row(row, fold):
    for group in range(fold.shape[0]):
        fold[group : group + 1, :] = row[:, group * LANES : (group + 1) * LANES]
    return fold[...]


def project_kernel(
    energy,
    hopping,
    potential_hbm,
    mode_energy_hbm,
    broadening_hbm,
    self_left_hbm,
    self_right_hbm,
    profile_hbm,
    profile,
    onsite_out,
    contact_out,
    run_out,
    potential,
    mode_energy,
    broadening,
    self_left,
    self_right,
    staged,
    fold,
    small_arrived,
    arrived,
):
    slabs = potential.shape[0]
    groups = profile.shape[0] // LANES
    small = []
    for place, (source, target) in enumerate(
        (
            (potential_hbm, potential),
            (mode_energy_hbm, mode_energy),
            (broadening_hbm, broadening),
            (self_left_hbm, self_left),
            (self_right_hbm, self_right),
        )
    ):
        small.append(pltpu.make_async_copy(source, target, small_arrived.at[place]))
        small[-1].start()
    copies = []
    for group in range(groups):
        rows = pl.ds(group * LANES, LANES)
        copies.append(
            pltpu.make_async_copy(profile_hbm.at[0, rows], profile.at[rows], arrived.at[group])
        )
        copies[-1].start()
    for copy in small:
        copy.wait()
    inverse = 1.0 / jnp.full((groups, LANES), hopping[0], jnp.float32)
    level = (energy[0] - fold_row(mode_energy, fold.at[0])) * inverse
    damping = fold_row(broadening, fold.at[1]) * inverse
    onsite_out[slabs] = damping
    onsite_out[slabs + 1] = inverse
    for part in range(2):
        contact_out[part] = fold_row(self_left.at[0, part : part + 1], fold.at[2 + part]) * inverse
        contact_out[2 + part] = (
            fold_row(self_right.at[0, part : part + 1], fold.at[4 + part]) * inverse
        )
    for group in range(groups):
        copies[group].wait()
        staged[group * slabs : (group + 1) * slabs, :] = lax.dot_general(
            potential[...],
            profile[group * LANES : (group + 1) * LANES, :],
            (((1,), (1,)), ((), ())),
            preferred_element_type=jnp.float32,
        )
    runs = []
    length = math.gcd(slabs, 4)
    for start in range(0, slabs, length):
        run = None
        for slab in range(start, start + length):
            real = level - staged[pl.ds(slab, groups, stride=slabs), :] * inverse
            onsite_out[slab] = real
            onsite = (real, damping)
            if run is None:
                alone = invert(onsite)
                run = (alone, alone, times(alone, alone))
            else:
                run = extend(run, onsite)
        runs.append(run)
    while len(runs) > 1:
        paired = [join(runs[k], runs[k + 1]) for k in range(0, len(runs) - 1, 2)]
        runs = paired + runs[2 * len(paired) :]
    for place, part in enumerate(part for pair in runs[0] for part in pair):
        run_out[place] = part


def charge_kernel(
    reach,
    occupation,
    onsite_in,
    outer_in,
    inner_run,
    sent_in,
    profile,
    charge_hbm,
    *rest,
):
    densities, (staged, charge, half, leaving) = rest[:-4], rest[-4:]
    slabs = charge.shape[1]
    groups = onsite_in.shape[1]
    outer = (outer_in[0], outer_in[1])
    inner = carry(
        tuple((inner_run[2 * k], inner_run[2 * k + 1]) for k in range(3)), (sent_in[0], sent_in[1])
    )
    is_upper = (lax.axis_index("slab") & reach) > 0
    left = pick(is_upper, inner, outer)
    right = pick(is_upper, outer, inner)
    damping = onsite_in[slabs]
    weight = (occupation[0] / math.pi) * onsite_in[slabs + 1]
    lefts, rights = [left], [right]
    for slab in range(slabs - 1):
        lefts.append(invert(minus((onsite_in[slab], damping), lefts[-1])))
        rights.append(invert(minus((onsite_in[slabs - 1 - slab], damping), rights[-1])))
    for slab in range(slabs):
        below = minus((onsite_in[slab], damping), plus(lefts[slab], rights[slabs - 1 - slab]))
        staged[pl.ds(slab, groups, stride=slabs), :] = (
            weight * below[1] / (below[0] * below[0] + below[1] * below[1])
        )
    for group in range(groups):
        columns = slice(group * LANES, (group + 1) * LANES)
        rows = staged[group * slabs : (group + 1) * slabs, :]
        charge[0, :, columns] = rows
        half[:, columns] = rows.astype(jnp.bfloat16)
    copy = pltpu.make_async_copy(charge, charge_hbm, leaving)
    copy.start()
    blocks = len(densities)
    block = lax.axis_index("blk")
    valleys, piece = densities[0].shape[0], densities[0].shape[2]
    for shift in reversed(range(blocks)):
        owner = lax.rem(block + shift, blocks)
        for valley in range(valleys):
            start = pl.multiple_of((valley * blocks + owner) * piece, piece)
            densities[shift][valley] = jnp.dot(
                half[...], profile[:, pl.ds(start, piece)], preferred_element_type=jnp.float32
            )
    copy.wait()


def alone_like(run):
    zero = jnp.zeros_like(run[0])
    return ((zero, zero), (zero, zero), (zero + 1.0, zero))


def widen(reach, group, other, before=None, after=None):
    is_second = (lax.axis_index("slab") & reach) > 0
    group, other = unpack(group), unpack(other)
    nothing = alone_like(group[0])
    if before is None:
        before, after = pick(is_second, other, nothing), pick(is_second, nothing, other)
    else:
        before, after = unpack(before), unpack(after)
        before, after = (
            pick(is_second, join(other, before), before),
            pick(is_second, after, join(after, other)),
        )
    group = join(pick(is_second, other, group), pick(is_second, group, other))
    return pack(group), pack(before), pack(after)


def close(reach, contact, group, before=None, after=None):
    is_upper = (lax.axis_index("slab") & reach) > 0
    group = unpack(group)
    nothing = alone_like(group[0])
    before = nothing if before is None else unpack(before)
    after = nothing if after is None else unpack(after)
    left_end, right_end = unpack(contact)
    end = pick(is_upper, right_end, left_end)
    sent = carry(pick(is_upper, flip(group), group), end)
    outer = carry(pick(is_upper, flip(after), before), end)
    inner_run = pick(is_upper, before, flip(after))
    return pack((sent,)), pack((outer,)), pack(inner_run)


def settle(reach, contact, *runs):
    return close(2 * reach, contact, *widen(reach, *runs))


def split_valleys(mine, *arrived):
    total = mine
    for part in arrived:
        total = total + part
    valleys = mine.shape[0]
    valley = lax.axis_index("valley")
    pieces = []
    for shift in range(valleys):
        owner = lax.rem(valley + shift, valleys)
        piece = total[0]
        for other in range(1, valleys):
            piece = jnp.where(owner == other, total[other], piece)
        pieces.append(piece)
    return tuple(pieces)


def on_vmem(function, *arrays):
    def kernel(*refs):
        results = function(*(ref[...] for ref in refs[: len(arrays)]))
        for ref, result in zip(refs[len(arrays) :], results, strict=True):
            ref[...] = result

    shapes = jax.eval_shape(function, *arrays)
    vmem = pl.BlockSpec(memory_space=pltpu.VMEM)
    return pl.pallas_call(
        kernel,
        out_shape=shapes,
        in_specs=[vmem] * len(arrays),
        out_specs=jax.tree.map(lambda shape: vmem, shapes),
        compiler_params=pltpu.CompilerParams(vmem_limit_bytes=SMALL_LIMIT),
    )(*arrays)


def body(
    potential,
    mode_density,
    energy,
    hopping,
    mode_energy,
    broadening,
    self_left,
    self_right,
    occupation,
):
    slabs, width = potential.shape
    modes = mode_density.shape[1]
    groups = modes // LANES
    smem = pl.BlockSpec(memory_space=pltpu.SMEM)
    vmem = pl.BlockSpec(memory_space=pltpu.VMEM)
    hbm = pl.BlockSpec(memory_space=pltpu.HBM)
    f32 = jnp.float32
    small = (potential, mode_energy, broadening, self_left, self_right)
    in_hbm = [
        pltpu.with_memory_space_constraint(array, pltpu.HBM) for array in (*small, mode_density)
    ]
    profile, onsite, contact, run = pl.pallas_call(
        project_kernel,
        out_shape=(
            jax.ShapeDtypeStruct((modes, width), mode_density.dtype),
            jax.ShapeDtypeStruct((slabs + 2, groups, LANES), f32),
            jax.ShapeDtypeStruct((4, groups, LANES), f32),
            jax.ShapeDtypeStruct((6, groups, LANES), f32),
        ),
        in_specs=[smem, smem] + [hbm] * (len(small) + 1),
        out_specs=(vmem, vmem, vmem, vmem),
        scratch_shapes=[pltpu.VMEM(array.shape, array.dtype) for array in small]
        + [
            pltpu.VMEM((groups * slabs, LANES), f32),
            pltpu.VMEM((6, groups, LANES), f32),
            pltpu.SemaphoreType.DMA((len(small),)),
            pltpu.SemaphoreType.DMA((groups,)),
        ],
        compiler_params=pltpu.CompilerParams(vmem_limit_bytes=VMEM_LIMIT),
        cost_estimate=pl.CostEstimate(
            flops=2 * slabs * width * modes, bytes_accessed=2 * width * modes, transcendentals=0
        ),
    )(energy, hopping, *in_hbm)

    count = lax.axis_size("slab")
    around = ()
    group = run
    reach = 1
    while 2 * reach < count:
        other = lax.ppermute(group, "slab", [(k, k ^ reach) for k in range(count)])
        if 4 * reach < count:
            group, *around = on_vmem(functools.partial(widen, reach), group, other, *around)
        else:
            sent, outer, inner_run = on_vmem(
                functools.partial(settle, reach), contact, group, other, *around
            )
        reach *= 2
    if count <= 2:
        sent, outer, inner_run = on_vmem(functools.partial(close, reach), contact, group)
    if count > 1:
        sent = lax.ppermute(sent, "slab", [(k, k ^ reach) for k in range(count)])
    else:
        sent = contact[2:]

    valleys, blocks = lax.axis_size("valley"), lax.axis_size("blk")
    piece = width // (valleys * blocks)
    charge, *terms = pl.pallas_call(
        functools.partial(charge_kernel, reach),
        out_shape=[jax.ShapeDtypeStruct((1, slabs, modes), f32)]
        + [jax.ShapeDtypeStruct((valleys, slabs, piece), f32)] * blocks,
        in_specs=[smem] + [vmem] * 5,
        out_specs=[hbm] + [vmem] * blocks,
        scratch_shapes=[
            pltpu.VMEM((groups * slabs, LANES), f32),
            pltpu.VMEM((1, slabs, modes), f32),
            pltpu.VMEM((slabs, modes), jnp.bfloat16),
            pltpu.SemaphoreType.DMA,
        ],
        compiler_params=pltpu.CompilerParams(vmem_limit_bytes=VMEM_LIMIT),
        cost_estimate=pl.CostEstimate(
            flops=2 * slabs * width * modes, bytes_accessed=2 * width * modes, transcendentals=0
        ),
    )(occupation, onsite, outer, inner_run, sent, profile)

    arrived = [
        lax.ppermute(terms[shift], "blk", [(k, (k + shift) % blocks) for k in range(blocks)])
        for shift in range(1, blocks)
    ]
    density, *away = on_vmem(split_valleys, terms[0], *arrived)
    for shift in range(1, valleys):
        pairs = [(k, (k + shift) % valleys) for k in range(valleys)]
        density = density + lax.ppermute(away[shift - 1], "valley", pairs)
    return charge, density


def solution(mesh):
    placed = (
        P("slab", None),
        P(("parts", "valley"), "blk", None),
        P(("parts", "valley")),
        P(("parts", "valley")),
        P(("parts", "valley"), "blk"),
        P(("parts", "valley"), "blk"),
        P(("parts", "valley"), None, "blk"),
        P(("parts", "valley"), None, "blk"),
        P(("parts", "valley")),
    )
    return jax.shard_map(
        body,
        mesh=mesh,
        in_specs=placed,
        out_specs=(P(("parts", "valley"), "slab", "blk"), P(("parts", "slab"), ("valley", "blk"))),
        check_vma=False,
    )
```

time: 31.3 us -> 23.8 us (0.76)
  local copies, waits for them, and re-layouts: 8.23 us -> 0 us
  Pallas kernels: 4.94 us -> 6.14 us
    unnamed x15 -> x0, local copies, waits for them, and re-layouts: 7.99 us -> none
    pallas_call x2 -> x4, Pallas kernels: 4.94 us -> 6.14 us  [the longest x1 5.23 us: body(): pl.pallas_call(project_kernel, out_shape=(jax.ShapeDtypeStruct((modes, wi...]
    ppermute x3, waiting for transfers between devices: 4.47 us -> 5.14 us  [the longest x1 2.09 us: body(): density = density + lax.ppermute(away[shift - 1], 'valley', pairs)]
    ppermute x1, waiting for transfers between devices: 1.61 us -> 0.98 us  [body(): sent = lax.ppermute(sent, 'slab', [(k, k ^ reach) for k in range(count)])]
    reshape x1 -> x0, other arithmetic: 0.62 us -> none  [body(): return (charge, terms.reshape(slabs, piece))]
    add x3 -> x1, other arithmetic: 0.08 us -> 0.62 us  [body(): density = density + lax.ppermute(away[shift - 1], 'valley', pairs)]
where the time goes in v2:
time: 23.8 us; the launch traced here: 23.6 us
  starting transfers between devices  8.14 us (34%)
  Pallas kernels  6.14 us (26%)
  waiting for transfers between devices  6.12 us (26%)
  between operations  2.61 us (11%)
  other arithmetic  0.62 us (3%)
    pallas_call x1, Pallas kernels, body(): pl.pallas_call(project_kernel, out_shape=(jax.ShapeDtypeStruct((modes, wi...  5.23 us
    ppermute x1, starting transfers between devices, body(): sent = lax.ppermute(sent, 'slab', [(k, k ^ reach) for k in range(count)])  3.1 us
    ppermute x1, starting transfers between devices, body(): other = lax.ppermute(group, 'slab', [(k, k ^ reach) for k in range(count)])  3.09 us
    ppermute x1, waiting for transfers between devices, body(): density = density + lax.ppermute(away[shift - 1], 'valley', pairs)  2.09 us
    ppermute x1, starting transfers between devices, body(): density = density + lax.ppermute(away[shift - 1], 'valley', pairs)  1.89 us
    ppermute x1, waiting for transfers between devices, body(): other = lax.ppermute(group, 'slab', [(k, k ^ reach) for k in range(count)])  1.81 us
    ppermute x1, waiting for transfers between devices, body(): lax.ppermute(terms[shift], 'blk', [(k, (k + shift) % blocks) for k in ran...  1.24 us
    ppermute x1, waiting for transfers between devices, body(): sent = lax.ppermute(sent, 'slab', [(k, k ^ reach) for k in range(count)])  0.98 us
  transfers between devices with their start and end apart: 4, of which 4 were waited for; matrix products, arithmetic and copies ran while one was open for 0% of the time, Pallas kernels for 0%

profile of v2, /device:TPU:0, one launch (start us, length us, event | category | flops | bytes accessed | tf_op | source)
XLA Modules:
  0.0 23.6 jit_solution(10625487686191581566)
XLA Ops:
  1.9 5.2 %shard_map.104 = (bf16[1024,2048]{1,0:T(8,128)(2,1)S(1)}, f32[18,8,128]{2,1,0:T(8,128)S(1)}, f32[4,8,128]{2,1,0:T(8,128)S(1)}, f32[6,8,128]{2,1,0:T(8,128)S(1)}) custom-call(f32[1]{0:T(128)S(6)} %copy.11.energy, f32[1]{0:T(128)S(6)} %copy.12.hopping, bf16[16,2048]{1,0:T(8,128)(2,1)} %potential_hbm.1, f32[1,1024]{1,0:T(1,128)} %mode_energy_hbm.1, ...), custom_call_target="tpu_custom_call" | custom-call | flops 67108864 | bytes 4194304 | tf_op jit(solution)/shard_map/pallas_call | solution.py:319
  7.2 3.1 %collective-permute-start = (f32[6,8,128]{2,1,0:T(8,128)S(1)}, f32[6,8,128]{2,1,0:T(8,128)S(1)}, u32[]{:S(2)}, u32[]{:S(2)}) collective-permute-start(f32[6,8,128]{2,1,0:T(8,128)S(1)} %get-tuple-element.16.refs_1_), channel_id=1, source_target_pairs={{0,4},{4,0},{8,12},{12,8},{1,5},{5,1},{9,13},{13,9},{2,6},{6,2},{1... | collective-permute-start | bytes 73736 | tf_op jit(solution)/shard_map/ppermute | solution.py:347
  10.2 1.8 %collective-permute-done.refs_2_ = f32[6,8,128]{2,1,0:T(8,128)S(1)} collective-permute-done((f32[6,8,128]{2,1,0:T(8,128)S(1)}, f32[6,8,128]{2,1,0:T(8,128)S(1)}, u32[]{:S(2)}, u32[]{:S(2)}) %collective-permute-start) | collective-permute-done | bytes 24608 | tf_op jit(solution)/shard_map/ppermute | solution.py:347
  12.1 3.1 %collective-permute-start.1 = (f32[2,8,128]{2,1,0:T(8,128)S(1)}, f32[2,8,128]{2,1,0:T(8,128)S(1)}, u32[]{:S(2)}, u32[]{:S(2)}) collective-permute-start(f32[2,8,128]{2,1,0:T(8,128)S(1)} %get-tuple-element.19), channel_id=1, source_target_pairs={{0,8},{4,12},{8,0},{12,4},{1,9},{5,13},{9,1},{13,5},{2,10},{6,14},... | collective-permute-start | bytes 24584 | tf_op jit(solution)/shard_map/ppermute | solution.py:358
  15.8 1.0 %collective-permute-done.1.sent_in = f32[2,8,128]{2,1,0:T(8,128)S(1)} collective-permute-done((f32[2,8,128]{2,1,0:T(8,128)S(1)}, f32[2,8,128]{2,1,0:T(8,128)S(1)}, u32[]{:S(2)}, u32[]{:S(2)}) %collective-permute-start.1) | collective-permute-done | bytes 8224 | tf_op jit(solution)/shard_map/ppermute | solution.py:358
  16.8 0.9 %shard_map.106 = (f32[1,16,1024]{2,1,0:T(8,128)}, f32[2,16,512]{2,1,0:T(8,128)S(1)}, f32[2,16,512]{2,1,0:T(8,128)S(1)}) custom-call(f32[1]{0:T(128)S(6)} %copy.13.occupation, f32[18,8,128]{2,1,0:T(8,128)S(1)} %get-tuple-element.14.onsite_in, f32[2,8,128]{2,1,0:T(8,128)S(1)} %get-tuple-element.17.outer_in, f32[6,8,128]{2,1,0:T(8,128)S(1)} %get-tuple-element.18.inner_run, ...), custom_call_target="tpu_custom_call" | custom-call | flops 67108864 | bytes 4194304 | tf_op jit(solution)/shard_map/pallas_call | solution.py:364
  17.7 0.1 collective-permute-start.2
  17.8 1.2 %collective-permute-done.2.refs_1_ = f32[2,16,512]{2,1,0:T(8,128)S(1)} collective-permute-done((f32[2,16,512]{2,1,0:T(8,128)S(1)}, f32[2,16,512]{2,1,0:T(8,128)S(1)}, u32[]{:S(2)}, u32[]{:S(2)}) %collective-permute-start.2) | collective-permute-done | bytes 65568 | tf_op jit(solution)/shard_map/ppermute | solution.py:383
  19.0 1.9 %collective-permute-start.3 = (f32[16,512]{1,0:T(8,128)S(1)}, f32[16,512]{1,0:T(8,128)S(1)}, u32[]{:S(2)}, u32[]{:S(2)}) collective-permute-start(f32[16,512]{1,0:T(8,128)S(1)} %get-tuple-element.25), channel_id=1, source_target_pairs={{0,2},{2,0},{1,3},{3,1},{4,6},{6,4},{5,7},{7,5},{8,10},{10,8},{9,1... | collective-permute-start | bytes 98312 | tf_op jit(solution)/shard_map/ppermute | solution.py:389
  20.9 2.1 %collective-permute-done.3 = f32[16,512]{1,0:T(8,128)S(1)} collective-permute-done((f32[16,512]{1,0:T(8,128)S(1)}, f32[16,512]{1,0:T(8,128)S(1)}, u32[]{:S(2)}, u32[]{:S(2)}) %collective-permute-start.3) | collective-permute-done | bytes 32800 | tf_op jit(solution)/shard_map/ppermute | solution.py:389
  23.0 0.6 %add.3 = f32[16,512]{1,0:T(8,128)} add(f32[16,512]{1,0:T(8,128)S(1)} %get-tuple-element.24, f32[16,512]{1,0:T(8,128)S(1)} %collective-permute-done.3) | non-fusion elementwise | flops 8192 | bytes 98304 | tf_op jit(solution)/shard_map/add | solution.py:389
  (2 shorter events, 0.0 us)
Async XLA Ops:
  7.2 4.9 %collective-permute-start = (f32[6,8,128]{2,1,0:T(8,128)S(1)}, f32[6,8,128]{2,1,0:T(8,128)S(1)}, u32[]{:S(2)}, u32[]{:S(2)}) collective-permute-start(f32[6,8,128]{2,1,0:T(8,128)S(1)} %get-tuple-element.16.refs_1_), channel_id=1, source_target_pairs={{0,4},{4,0},{8,12},{12,8},{1,5},{5,1},{9,13},{13,9},{2,6},{6,2},{1... | collective-permute-start | bytes 73736 | tf_op jit(solution)/shard_map/ppermute | solution.py:347
  12.1 4.7 %collective-permute-start.1 = (f32[2,8,128]{2,1,0:T(8,128)S(1)}, f32[2,8,128]{2,1,0:T(8,128)S(1)}, u32[]{:S(2)}, u32[]{:S(2)}) collective-permute-start(f32[2,8,128]{2,1,0:T(8,128)S(1)} %get-tuple-element.19), channel_id=1, source_target_pairs={{0,8},{4,12},{8,0},{12,4},{1,9},{5,13},{9,1},{13,5},{2,10},{6,14},... | collective-permute-start | bytes 24584 | tf_op jit(solution)/shard_map/ppermute | solution.py:358
  17.7 1.3 %collective-permute-start.2 = (f32[2,16,512]{2,1,0:T(8,128)S(1)}, f32[2,16,512]{2,1,0:T(8,128)S(1)}, u32[]{:S(2)}, u32[]{:S(2)}) collective-permute-start(f32[2,16,512]{2,1,0:T(8,128)S(1)} %get-tuple-element.23), channel_id=1, source_target_pairs={{0,1},{1,0},{2,3},{3,2},{4,5},{5,4},{6,7},{7,6},{8,9},{9,8},{10,11... | collective-permute-start | bytes 196616 | tf_op jit(solution)/shard_map/ppermute | solution.py:383
  19.0 4.0 %collective-permute-start.3 = (f32[16,512]{1,0:T(8,128)S(1)}, f32[16,512]{1,0:T(8,128)S(1)}, u32[]{:S(2)}, u32[]{:S(2)}) collective-permute-start(f32[16,512]{1,0:T(8,128)S(1)} %get-tuple-element.25), channel_id=1, source_target_pairs={{0,2},{2,0},{1,3},{3,1},{4,6},{6,4},{5,7},{7,5},{8,10},{10,8},{9,1... | collective-permute-start | bytes 98312 | tf_op jit(solution)/shard_map/ppermute | solution.py:389

commit v3 on v2

--- a/solution.py
+++ b/solution.py
@@ -85,70 +85,49 @@
     return fold[...]
 
 
+def scalar_kernel(energy, hopping, level_out):
+    level_out[0] = jnp.full(level_out.shape[1:], energy[0], jnp.float32)
+    level_out[1] = 1.0 / jnp.full(level_out.shape[1:], hopping[0], jnp.float32)
+
+
 def project_kernel(
-    energy,
-    hopping,
-    potential_hbm,
-    mode_energy_hbm,
-    broadening_hbm,
-    self_left_hbm,
-    self_right_hbm,
-    profile_hbm,
-    profile,
-    onsite_out,
-    contact_out,
-    run_out,
+    level_in,
     potential,
     mode_energy,
     broadening,
     self_left,
     self_right,
+    profile,
+    onsite_out,
+    contact_out,
+    run_out,
     staged,
     fold,
-    small_arrived,
-    arrived,
 ):
     slabs = potential.shape[0]
-    groups = profile.shape[0] // LANES
-    small = []
-    for place, (source, target) in enumerate(
-        (
-            (potential_hbm, potential),
-            (mode_energy_hbm, mode_energy),
-            (broadening_hbm, broadening),
-            (self_left_hbm, self_left),
-            (self_right_hbm, self_right),
-        )
-    ):
-        small.append(pltpu.make_async_copy(source, target, small_arrived.at[place]))
-        small[-1].start()
-    copies = []
-    for group in range(groups):
-        rows = pl.ds(group * LANES, LANES)
-        copies.append(
-            pltpu.make_async_copy(profile_hbm.at[0, rows], profile.at[rows], arrived.at[group])
-        )
-        copies[-1].start()
-    for copy in small:
-        copy.wait()
-    inverse = 1.0 / jnp.full((groups, LANES), hopping[0], jnp.float32)
-    level = (energy[0] - fold_row(mode_energy, fold.at[0])) * inverse
+    modes = profile.shape[1]
+    groups = modes // LANES
+    inverse = level_in[1]
+    level = (level_in[0] - fold_row(mode_energy, fold.at[0])) * inverse
     damping = fold_row(broadening, fold.at[1]) * inverse
-    onsite_out[slabs] = damping
-    onsite_out[slabs + 1] = inverse
     for part in range(2):
         contact_out[part] = fold_row(self_left.at[0, part : part + 1], fold.at[2 + part]) * inverse
         contact_out[2 + part] = (
             fold_row(self_right.at[0, part : part + 1], fold.at[4 + part]) * inverse
         )
-    for group in range(groups):
-        copies[group].wait()
-        staged[group * slabs : (group + 1) * slabs, :] = lax.dot_general(
+    onsite_out[slabs] = damping
+    onsite_out[slabs + 1] = inverse
+    chunk = math.gcd(modes, 256)
+    for start in range(0, modes, chunk):
+        result = lax.dot_general(
             potential[...],
-            profile[group * LANES : (group + 1) * LANES, :],
+            profile[0, start : start + chunk, :],
             (((1,), (1,)), ((), ())),
             preferred_element_type=jnp.float32,
         )
+        for column in range(0, chunk, LANES):
+            group = (start + column) // LANES
+            staged[group * slabs : (group + 1) * slabs, :] = result[:, column : column + LANES]
     runs = []
     length = math.gcd(slabs, 4)
     for start in range(0, slabs, length):
@@ -170,18 +149,31 @@
         run_out[place] = part
 
 
+def multiply(half, profile, term, valleys, blocks, valley_shifts, block_shift):
+    piece = term.shape[2]
+    owner_block = lax.rem(lax.axis_index("blk") + block_shift, blocks)
+    for place, shift in enumerate(valley_shifts):
+        owner_valley = lax.rem(lax.axis_index("valley") + shift, valleys)
+        start = pl.multiple_of((owner_valley * blocks + owner_block) * piece, piece)
+        term[place] = jnp.dot(
+            half[...], profile[0, :, pl.ds(start, piece)], preferred_element_type=jnp.float32
+        )
+
+
 def charge_kernel(
     reach,
+    plan,
     occupation,
     onsite_in,
     outer_in,
     inner_run,
     sent_in,
     profile,
-    charge_hbm,
+    charge,
+    half,
     *rest,
 ):
-    densities, (staged, charge, half, leaving) = rest[:-4], rest[-4:]
+    terms, staged = rest[:-1], rest[-1]
     slabs = charge.shape[1]
     groups = onsite_in.shape[1]
     outer = (outer_in[0], outer_in[1])
@@ -207,18 +199,19 @@
         rows = staged[group * slabs : (group + 1) * slabs, :]
         charge[0, :, columns] = rows
         half[:, columns] = rows.astype(jnp.bfloat16)
+    for term, block_shift in zip(terms, range(1, plan[1]), strict=True):
+        multiply(half, profile, term, *plan, block_shift)
+
+
+def term_kernel(plan, block_shifts, half, profile, *rest):
+    for term, block_shift in zip(rest[-len(block_shifts) :], block_shifts, strict=True):
+        multiply(half, profile, term, *plan, block_shift)
+
+
+def store_kernel(plan, half, profile, charge, after, term, charge_hbm, leaving):
     copy = pltpu.make_async_copy(charge, charge_hbm, leaving)
     copy.start()
-    blocks = len(densities)
-    block = lax.axis_index("blk")
-    valleys, piece = densities[0].shape[0], densities[0].shape[2]
-    for shift in reversed(range(blocks)):
-        owner = lax.rem(block + shift, blocks)
-        for valley in range(valleys):
-            start = pl.multiple_of((valley * blocks + owner) * piece, piece)
-            densities[shift][valley] = jnp.dot(
-                half[...], profile[:, pl.ds(start, piece)], preferred_element_type=jnp.float32
-            )
+    multiply(half, profile, term, *plan, 0)
     copy.wait()
 
 
@@ -261,20 +254,11 @@
     return close(2 * reach, contact, *widen(reach, *runs))
 
 
-def split_valleys(mine, *arrived):
+def add_blocks(mine, *arrived):
     total = mine
     for part in arrived:
         total = total + part
-    valleys = mine.shape[0]
-    valley = lax.axis_index("valley")
-    pieces = []
-    for shift in range(valleys):
-        owner = lax.rem(valley + shift, valleys)
-        piece = total[0]
-        for other in range(1, valleys):
-            piece = jnp.where(owner == other, total[other], piece)
-        pieces.append(piece)
-    return tuple(pieces)
+    return tuple(total[place] for place in range(mine.shape[0]))
 
 
 def on_vmem(function, *arrays):
@@ -310,34 +294,36 @@
     groups = modes // LANES
     smem = pl.BlockSpec(memory_space=pltpu.SMEM)
     vmem = pl.BlockSpec(memory_space=pltpu.VMEM)
-    hbm = pl.BlockSpec(memory_space=pltpu.HBM)
+    anywhere = pl.BlockSpec(memory_space=pl.ANY)
     f32 = jnp.float32
-    small = (potential, mode_energy, broadening, self_left, self_right)
-    in_hbm = [
-        pltpu.with_memory_space_constraint(array, pltpu.HBM) for array in (*small, mode_density)
-    ]
-    profile, onsite, contact, run = pl.pallas_call(
+    level = pl.pallas_call(
+        scalar_kernel,
+        out_shape=jax.ShapeDtypeStruct((2, groups, LANES), f32),
+        in_specs=[smem, smem],
+        out_specs=vmem,
+        compiler_params=pltpu.CompilerParams(vmem_limit_bytes=SMALL_LIMIT),
+        cost_estimate=pl.CostEstimate(
+            flops=600 * width * modes, bytes_accessed=8, transcendentals=0
+        ),
+    )(energy, hopping)
+    onsite, contact, run = pl.pallas_call(
         project_kernel,
         out_shape=(
-            jax.ShapeDtypeStruct((modes, width), mode_density.dtype),
             jax.ShapeDtypeStruct((slabs + 2, groups, LANES), f32),
             jax.ShapeDtypeStruct((4, groups, LANES), f32),
             jax.ShapeDtypeStruct((6, groups, LANES), f32),
         ),
-        in_specs=[smem, smem] + [hbm] * (len(small) + 1),
-        out_specs=(vmem, vmem, vmem, vmem),
-        scratch_shapes=[pltpu.VMEM(array.shape, array.dtype) for array in small]
-        + [
+        in_specs=[vmem] * 7,
+        out_specs=(vmem, vmem, vmem),
+        scratch_shapes=[
             pltpu.VMEM((groups * slabs, LANES), f32),
             pltpu.VMEM((6, groups, LANES), f32),
-            pltpu.SemaphoreType.DMA((len(small),)),
-            pltpu.SemaphoreType.DMA((groups,)),
         ],
         compiler_params=pltpu.CompilerParams(vmem_limit_bytes=VMEM_LIMIT),
         cost_estimate=pl.CostEstimate(
             flops=2 * slabs * width * modes, bytes_accessed=2 * width * modes, transcendentals=0
         ),
-    )(energy, hopping, *in_hbm)
+    )(level, potential, mode_energy, broadening, self_left, self_right, mode_density)
 
     count = lax.axis_size("slab")
     around = ()
@@ -361,32 +347,74 @@
 
     valleys, blocks = lax.axis_size("valley"), lax.axis_size("blk")
     piece = width // (valleys * blocks)
-    charge, *terms = pl.pallas_call(
-        functools.partial(charge_kernel, reach),
-        out_shape=[jax.ShapeDtypeStruct((1, slabs, modes), f32)]
-        + [jax.ShapeDtypeStruct((valleys, slabs, piece), f32)] * blocks,
+    away_plan = (valleys, blocks, tuple(range(1, valleys)))
+    home_plan = (valleys, blocks, (0,))
+
+    def term_shapes(plan, count):
+        return [jax.ShapeDtypeStruct((len(plan[2]), slabs, piece), f32)] * count
+
+    def cost(plan, count):
+        columns = len(plan[2]) * count * piece
+        return pl.CostEstimate(
+            flops=2 * slabs * columns * modes, bytes_accessed=2 * columns * modes, transcendentals=0
+        )
+
+    def swap(terms):
+        return [
+            lax.ppermute(term, "blk", [(k, (k + shift) % blocks) for k in range(blocks)])
+            for shift, term in enumerate(terms, 1)
+        ]
+
+    first_plan = away_plan if valleys > 1 else home_plan
+    charge, half, *others = pl.pallas_call(
+        functools.partial(charge_kernel, reach, first_plan),
+        out_shape=[
+            jax.ShapeDtypeStruct((1, slabs, modes), f32),
+            jax.ShapeDtypeStruct((slabs, modes), jnp.bfloat16),
+        ]
+        + term_shapes(first_plan, blocks - 1),
         in_specs=[smem] + [vmem] * 5,
-        out_specs=[hbm] + [vmem] * blocks,
-        scratch_shapes=[
-            pltpu.VMEM((groups * slabs, LANES), f32),
-            pltpu.VMEM((1, slabs, modes), f32),
-            pltpu.VMEM((slabs, modes), jnp.bfloat16),
-            pltpu.SemaphoreType.DMA,
-        ],
+        out_specs=[vmem] * (blocks + 1),
+        scratch_shapes=[pltpu.VMEM((groups * slabs, LANES), f32)],
         compiler_params=pltpu.CompilerParams(vmem_limit_bytes=VMEM_LIMIT),
-        cost_estimate=pl.CostEstimate(
-            flops=2 * slabs * width * modes, bytes_accessed=2 * width * modes, transcendentals=0
-        ),
-    )(occupation, onsite, outer, inner_run, sent, profile)
-
-    arrived = [
-        lax.ppermute(terms[shift], "blk", [(k, (k + shift) % blocks) for k in range(blocks)])
-        for shift in range(1, blocks)
-    ]
-    density, *away = on_vmem(split_valleys, terms[0], *arrived)
-    for shift in range(1, valleys):
-        pairs = [(k, (k + shift) % valleys) for k in range(valleys)]
-        density = density + lax.ppermute(away[shift - 1], "valley", pairs)
+        cost_estimate=cost(first_plan, blocks - 1),
+    )(occupation, onsite, outer, inner_run, sent, mode_density)
+
+    def terms_of(plan, block_shifts, *after):
+        return pl.pallas_call(
+            functools.partial(term_kernel, plan, block_shifts),
+            out_shape=term_shapes(plan, len(block_shifts)),
+            in_specs=[vmem] * 2 + [anywhere] * len(after),
+            out_specs=[vmem] * len(block_shifts),
+            compiler_params=pltpu.CompilerParams(vmem_limit_bytes=VMEM_LIMIT),
+            cost_estimate=cost(plan, len(block_shifts)),
+        )(half, mode_density, *after)
+
+    others = swap(others)
+    arrived = []
+    after = half
+    if valleys > 1:
+        away = on_vmem(add_blocks, *terms_of(away_plan, (0,)), *others)
+        after = away[0]
+        for shift in range(1, valleys):
+            pairs = [(k, (k + shift) % valleys) for k in range(valleys)]
+            arrived.append(lax.ppermute(away[shift - 1], "valley", pairs))
+        if blocks > 1:
+            others = swap(terms_of(home_plan, range(1, blocks), after))
+    term, charge = pl.pallas_call(
+        functools.partial(store_kernel, home_plan),
+        out_shape=term_shapes(home_plan, 1) + [jax.ShapeDtypeStruct(charge.shape, f32)],
+        in_specs=[vmem] * 3 + [anywhere],
+        out_specs=[vmem, anywhere],
+        scratch_shapes=[pltpu.SemaphoreType.DMA],
+        compiler_params=pltpu.CompilerParams(vmem_limit_bytes=VMEM_LIMIT),
+        cost_estimate=cost(home_plan, 1),
+    )(half, mode_density, charge, after)
+    density = term[0]
+    for part in others:
+        density = density + part[0]
+    for part in arrived:
+        density = density + part
     return charge, density
 
 

time: 23.8 us -> 20.3 us (0.85)
  Pallas kernels: 6.14 us -> 2.93 us
  waiting for transfers between devices: 6.12 us -> 4.94 us
  between operations: 2.61 us -> 3.29 us
  local copies, waits for them, and re-layouts: 0 us -> 0.33 us
    pallas_call x2 -> x6, Pallas kernels: 6.09 us -> 2.89 us  [the longest x1 1.31 us: body(): pl.pallas_call(project_kernel, out_shape=(jax.ShapeDtypeStruct((slabs + 2...]
    ppermute x2 -> x3, waiting for transfers between devices: 3.33 us -> 2.15 us  [the longest x1 1.19 us: body(): arrived.append(lax.ppermute(away[shift - 1], 'valley', pairs))]
    unnamed x0 -> x12, local copies, waits for them, and re-layouts: none -> 0.33 us
    ppermute x2 -> x3, starting transfers between devices: 1.96 us -> 1.83 us  [the longest x1 1.82 us: body(): arrived.append(lax.ppermute(away[shift - 1], 'valley', pairs))]
  transfers between devices with their start and end apart: 4 -> 5, of which waited for: 4 -> 4; matrix products, arithmetic and copies ran while one was open for 0% -> 0% of each run, Pallas kernels for 0% -> 6%
where the time goes in v3:
time: 20.3 us; the launch traced here: 20.1 us
  starting transfers between devices  8.01 us (39%)
  waiting for transfers between devices  4.94 us (24%)
  between operations  3.29 us (16%)
  Pallas kernels  2.93 us (14%)
  other arithmetic  0.62 us (3%)
  local copies, waits for them, and re-layouts  0.33 us (2%)
    ppermute x1, starting transfers between devices, body(): sent = lax.ppermute(sent, 'slab', [(k, k ^ reach) for k in range(count)])  3.1 us
    ppermute x1, starting transfers between devices, body(): other = lax.ppermute(group, 'slab', [(k, k ^ reach) for k in range(count)])  3.09 us
    ppermute x1, starting transfers between devices, body(): arrived.append(lax.ppermute(away[shift - 1], 'valley', pairs))  1.82 us
    ppermute x1, waiting for transfers between devices, body(): other = lax.ppermute(group, 'slab', [(k, k ^ reach) for k in range(count)])  1.81 us
    pallas_call x1, Pallas kernels, body(): pl.pallas_call(project_kernel, out_shape=(jax.ShapeDtypeStruct((slabs + 2...  1.31 us
    ppermute x1, waiting for transfers between devices, body(): arrived.append(lax.ppermute(away[shift - 1], 'valley', pairs))  1.19 us
    ppermute x1, waiting for transfers between devices, body(): sent = lax.ppermute(sent, 'slab', [(k, k ^ reach) for k in range(count)])  0.98 us
    ppermute x2, waiting for transfers between devices, swap(): lax.ppermute(term, 'blk', [(k, (k + shift) % blocks) for k in range(block...  0.97 us
  transfers between devices with their start and end apart: 5, of which 4 were waited for; matrix products, arithmetic and copies ran while one was open for 0% of the time, Pallas kernels for 6%

profile of v3, /device:TPU:0, one launch (start us, length us, event | category | flops | bytes accessed | tf_op | source)
XLA Modules:
  0.0 20.1 jit_solution(10983344239002062014)
XLA Ops:
  0.6 0.0 copy-start.1
  0.6 0.0 copy-start.4
  0.7 0.0 copy-start.5
  0.7 0.0 copy-start.2
  0.7 0.0 copy-start.3
  0.7 0.0 copy-start
  2.6 0.0 copy-done.1
  2.6 0.0 copy-done.4
  2.6 0.0 copy-done.5
  2.6 0.0 copy-done.2
  2.6 0.0 copy-done.3
  2.6 0.3 %copy-done = bf16[1,1024,2048]{2,1,0:T(8,128)(2,1)S(1)} copy-done((bf16[1,1024,2048]{2,1,0:T(8,128)(2,1)S(1)}, bf16[1,1024,2048]{2,1,0:T(8,128)(2,1)}, u32[]{:S(2)}) %copy-start) | copy-done | bytes 4194328
  3.0 1.3 %shard_map.105 = (f32[18,8,128]{2,1,0:T(8,128)S(1)}, f32[4,8,128]{2,1,0:T(8,128)S(1)}, f32[6,8,128]{2,1,0:T(8,128)S(1)}) custom-call(f32[2,8,128]{2,1,0:T(8,128)S(1)} %shard_map.104.level_in, bf16[16,2048]{1,0:T(8,128)(2,1)S(1)} %copy-done.1, f32[1,1024]{1,0:T(1,128)S(1)} %copy-done.4, f32[1,1024]{1,0:T(1,128)S(1)} %copy-done.5, ...), custom_call_target="tpu_custom_call" | custom-call | flops 67108864 | bytes 4194304 | tf_op jit(solution)/shard_map/pallas_call | solution.py:309
  4.3 3.1 %collective-permute-start = (f32[6,8,128]{2,1,0:T(8,128)S(1)}, f32[6,8,128]{2,1,0:T(8,128)S(1)}, u32[]{:S(2)}, u32[]{:S(2)}) collective-permute-start(f32[6,8,128]{2,1,0:T(8,128)S(1)} %get-tuple-element.15.refs_1_), channel_id=1, source_target_pairs={{0,4},{4,0},{8,12},{12,8},{1,5},{5,1},{9,13},{13,9},{2,6},{6,2},{1... | collective-permute-start | bytes 73736 | tf_op jit(solution)/shard_map/ppermute | solution.py:333
  7.4 1.8 %collective-permute-done.refs_2_ = f32[6,8,128]{2,1,0:T(8,128)S(1)} collective-permute-done((f32[6,8,128]{2,1,0:T(8,128)S(1)}, f32[6,8,128]{2,1,0:T(8,128)S(1)}, u32[]{:S(2)}, u32[]{:S(2)}) %collective-permute-start) | collective-permute-done | bytes 24608 | tf_op jit(solution)/shard_map/ppermute | solution.py:333
  9.2 3.1 %collective-permute-start.1 = (f32[2,8,128]{2,1,0:T(8,128)S(1)}, f32[2,8,128]{2,1,0:T(8,128)S(1)}, u32[]{:S(2)}, u32[]{:S(2)}) collective-permute-start(f32[2,8,128]{2,1,0:T(8,128)S(1)} %get-tuple-element.18), channel_id=1, source_target_pairs={{0,8},{4,12},{8,0},{12,4},{1,9},{5,13},{9,1},{13,5},{2,10},{6,14},... | collective-permute-start | bytes 24584 | tf_op jit(solution)/shard_map/ppermute | solution.py:344
  13.0 1.0 %collective-permute-done.1.sent_in = f32[2,8,128]{2,1,0:T(8,128)S(1)} collective-permute-done((f32[2,8,128]{2,1,0:T(8,128)S(1)}, f32[2,8,128]{2,1,0:T(8,128)S(1)}, u32[]{:S(2)}, u32[]{:S(2)}) %collective-permute-start.1) | collective-permute-done | bytes 8224 | tf_op jit(solution)/shard_map/ppermute | solution.py:344
  13.9 0.4 %shard_map.107 = (f32[1,16,1024]{2,1,0:T(8,128)S(1)}, bf16[16,1024]{1,0:T(8,128)(2,1)S(1)}, f32[1,16,512]{2,1,0:T(8,128)S(1)}) custom-call(f32[1]{0:T(128)S(6)} %copy.13.occupation, f32[18,8,128]{2,1,0:T(8,128)S(1)} %get-tuple-element.13.onsite_in, f32[2,8,128]{2,1,0:T(8,128)S(1)} %get-tuple-element.16.outer_in, ...), custom_call_target="tpu_custom_call" | custom-call | flops 16777216 | bytes 1048576 | tf_op jit(solution)/shard_map/pallas_call | solution.py:369
  14.4 0.0 collective-permute-start.2
  14.4 0.3 %shard_map.108.refs_0_ = f32[1,16,512]{2,1,0:T(8,128)S(1)} custom-call(bf16[16,1024]{1,0:T(8,128)(2,1)S(1)} %get-tuple-element.19.half, bf16[1,1024,2048]{2,1,0:T(8,128)(2,1)S(1)} %copy-done), custom_call_target="tpu_custom_call" | custom-call | flops 16777216 | bytes 1048576 | tf_op jit(solution)/shard_map/pallas_call | solution.py:384
  14.6 1.0 %collective-permute-done.2.refs_1_ = f32[1,16,512]{2,1,0:T(8,128)S(1)} collective-permute-done((f32[1,16,512]{2,1,0:T(8,128)S(1)}, f32[1,16,512]{2,1,0:T(8,128)S(1)}, u32[]{:S(2)}, u32[]{:S(2)}) %collective-permute-start.2) | collective-permute-done | bytes 32800 | tf_op jit(solution)/shard_map/ppermute | solution.py:364
  15.6 1.8 %collective-permute-start.4 = (f32[16,512]{1,0:T(8,128)S(1)}, f32[16,512]{1,0:T(8,128)S(1)}, u32[]{:S(2)}, u32[]{:S(2)}) collective-permute-start(f32[16,512]{1,0:T(8,128)S(1)} %shard_map.109.after.rest_0_), channel_id=1, source_target_pairs={{0,2},{2,0},{1,3},{3,1},{4,6},{6,4},{5,7},{7,5},{8,10},{10,8},{9,1... | collective-permute-start | bytes 98312 | tf_op jit(solution)/shard_map/ppermute | solution.py:401
  17.4 0.2 %shard_map.111 = f32[1,16,512]{2,1,0:T(8,128)S(1)} custom-call(bf16[16,1024]{1,0:T(8,128)(2,1)S(1)} %get-tuple-element.19.half, bf16[1,1024,2048]{2,1,0:T(8,128)(2,1)S(1)} %copy-done, f32[16,512]{1,0:T(8,128)S(1)} %shard_map.109.after.rest_0_), custom_call_target="tpu_custom_call" | custom-call | flops 16777216 | bytes 1048576 | tf_op jit(solution)/shard_map/pallas_call | solution.py:384
  17.6 0.0 collective-permute-start.3
  17.7 0.7 %shard_map.110 = (f32[1,16,512]{2,1,0:T(8,128)S(1)}, f32[1,16,1024]{2,1,0:T(8,128)}) custom-call(bf16[16,1024]{1,0:T(8,128)(2,1)S(1)} %get-tuple-element.19.half, bf16[1,1024,2048]{2,1,0:T(8,128)(2,1)S(1)} %copy-done, f32[1,16,1024]{2,1,0:T(8,128)S(1)} %get-tuple-element.20.charge, f32[16,512]{1,0:T(8,128)S(1)} %shard_map.109.after.rest_0_), custom_call_target="tpu_custom_call" | custom-call | flops 16777216 | bytes 1048576 | tf_op jit(solution)/shard_map/pallas_call | solution.py:404
  18.3 1.2 %collective-permute-done.4 = f32[16,512]{1,0:T(8,128)S(1)} collective-permute-done((f32[16,512]{1,0:T(8,128)S(1)}, f32[16,512]{1,0:T(8,128)S(1)}, u32[]{:S(2)}, u32[]{:S(2)}) %collective-permute-start.4) | collective-permute-done | bytes 32800 | tf_op jit(solution)/shard_map/ppermute | solution.py:401
  19.5 0.0 collective-permute-done.3
  19.5 0.6 %bitcast_add_fusion = f32[16,512]{1,0:T(8,128)} fusion(f32[16,512]{1,0:T(8,128)S(1)} %collective-permute-done.4, f32[1,16,512]{2,1,0:T(8,128)S(1)} %get-tuple-element.23, f32[1,16,512]{2,1,0:T(8,128)S(1)} %collective-permute-done.3), kind=kLoop, calls=%fused_computation | loop fusion | flops 16384 | bytes 131072 | tf_op jit(solution)/shard_map/add | solution.py:417
  (3 shorter events, 0.0 us)
Async XLA Ops:
  0.6 2.0 %copy-start.1 = (bf16[16,2048]{1,0:T(8,128)(2,1)S(1)}, bf16[16,2048]{1,0:T(8,128)(2,1)}, u32[]{:S(2)}) copy-start(bf16[16,2048]{1,0:T(8,128)(2,1)} %potential.1) | copy-start | bytes 196612
  0.6 2.0 %copy-start.4 = (f32[1,1024]{1,0:T(1,128)S(1)}, f32[1,1024]{1,0:T(1,128)}, u32[]{:S(2)}) copy-start(f32[1,1024]{1,0:T(1,128)} %mode_energy.1) | copy-start | bytes 12292
  0.7 2.0 %copy-start.5 = (f32[1,1024]{1,0:T(1,128)S(1)}, f32[1,1024]{1,0:T(1,128)}, u32[]{:S(2)}) copy-start(f32[1,1024]{1,0:T(1,128)} %broadening.1) | copy-start | bytes 12292
  0.7 2.0 %copy-start.2 = (f32[1,2,1024]{2,1,0:T(2,128)S(1)}, f32[1,2,1024]{2,1,0:T(2,128)}, u32[]{:S(2)}) copy-start(f32[1,2,1024]{2,1,0:T(2,128)} %self_left.1) | copy-start | bytes 24580
  0.7 2.0 %copy-start.3 = (f32[1,2,1024]{2,1,0:T(2,128)S(1)}, f32[1,2,1024]{2,1,0:T(2,128)}, u32[]{:S(2)}) copy-start(f32[1,2,1024]{2,1,0:T(2,128)} %self_right.1) | copy-start | bytes 24580
  0.7 2.3 %copy-start = (bf16[1,1024,2048]{2,1,0:T(8,128)(2,1)S(1)}, bf16[1,1024,2048]{2,1,0:T(8,128)(2,1)}, u32[]{:S(2)}) copy-start(bf16[1,1024,2048]{2,1,0:T(8,128)(2,1)} %profile.9) | copy-start | bytes 12582916
  4.3 4.9 %collective-permute-start = (f32[6,8,128]{2,1,0:T(8,128)S(1)}, f32[6,8,128]{2,1,0:T(8,128)S(1)}, u32[]{:S(2)}, u32[]{:S(2)}) collective-permute-start(f32[6,8,128]{2,1,0:T(8,128)S(1)} %get-tuple-element.15.refs_1_), channel_id=1, source_target_pairs={{0,4},{4,0},{8,12},{12,8},{1,5},{5,1},{9,13},{13,9},{2,6},{6,2},{1... | collective-permute-start | bytes 73736 | tf_op jit(solution)/shard_map/ppermute | solution.py:333
  9.2 4.7 %collective-permute-start.1 = (f32[2,8,128]{2,1,0:T(8,128)S(1)}, f32[2,8,128]{2,1,0:T(8,128)S(1)}, u32[]{:S(2)}, u32[]{:S(2)}) collective-permute-start(f32[2,8,128]{2,1,0:T(8,128)S(1)} %get-tuple-element.18), channel_id=1, source_target_pairs={{0,8},{4,12},{8,0},{12,4},{1,9},{5,13},{9,1},{13,5},{2,10},{6,14},... | collective-permute-start | bytes 24584 | tf_op jit(solution)/shard_map/ppermute | solution.py:344
  14.4 1.2 %collective-permute-start.2 = (f32[1,16,512]{2,1,0:T(8,128)S(1)}, f32[1,16,512]{2,1,0:T(8,128)S(1)}, u32[]{:S(2)}, u32[]{:S(2)}) collective-permute-start(f32[1,16,512]{2,1,0:T(8,128)S(1)} %get-tuple-element.21), channel_id=1, source_target_pairs={{0,1},{1,0},{2,3},{3,2},{4,5},{5,4},{6,7},{7,6},{8,9},{9,8},{10,11... | collective-permute-start | bytes 98312 | tf_op jit(solution)/shard_map/ppermute | solution.py:364
  15.6 3.9 %collective-permute-start.4 = (f32[16,512]{1,0:T(8,128)S(1)}, f32[16,512]{1,0:T(8,128)S(1)}, u32[]{:S(2)}, u32[]{:S(2)}) collective-permute-start(f32[16,512]{1,0:T(8,128)S(1)} %shard_map.109.after.rest_0_), channel_id=1, source_target_pairs={{0,2},{2,0},{1,3},{3,1},{4,6},{6,4},{5,7},{7,5},{8,10},{10,8},{9,1... | collective-permute-start | bytes 98312 | tf_op jit(solution)/shard_map/ppermute | solution.py:401
  17.6 1.9 %collective-permute-start.3 = (f32[1,16,512]{2,1,0:T(8,128)S(1)}, f32[1,16,512]{2,1,0:T(8,128)S(1)}, u32[]{:S(2)}, u32[]{:S(2)}) collective-permute-start(f32[1,16,512]{2,1,0:T(8,128)S(1)} %shard_map.111), channel_id=1, source_target_pairs={{0,1},{1,0},{2,3},{3,2},{4,5},{5,4},{6,7},{7,6},{8,9},{9,8},{10,11... | collective-permute-start | bytes 98312 | tf_op jit(solution)/shard_map/ppermute | solution.py:364

commit v4 on v3

--- a/solution.py
+++ b/solution.py
@@ -83,6 +83,12 @@
     for group in range(fold.shape[0]):
         fold[group : group + 1, :] = row[:, group * LANES : (group + 1) * LANES]
     return fold[...]
+
+
+def contract(first, second):
+    return lax.dot_general(
+        first, second, (((1,), (1,)), ((), ())), preferred_element_type=jnp.float32
+    )
 
 
 def scalar_kernel(energy, hopping, level_out):
@@ -105,8 +111,7 @@
     fold,
 ):
     slabs = potential.shape[0]
-    modes = profile.shape[1]
-    groups = modes // LANES
+    groups = run_out.shape[1]
     inverse = level_in[1]
     level = (level_in[0] - fold_row(mode_energy, fold.at[0])) * inverse
     damping = fold_row(broadening, fold.at[1]) * inverse
@@ -117,17 +122,22 @@
         )
     onsite_out[slabs] = damping
     onsite_out[slabs + 1] = inverse
-    chunk = math.gcd(modes, 256)
-    for start in range(0, modes, chunk):
-        result = lax.dot_general(
-            potential[...],
-            profile[0, start : start + chunk, :],
-            (((1,), (1,)), ((), ())),
-            preferred_element_type=jnp.float32,
-        )
-        for column in range(0, chunk, LANES):
-            group = (start + column) // LANES
-            staged[group * slabs : (group + 1) * slabs, :] = result[:, column : column + LANES]
+    split = groups // 2 * LANES
+    width = profile.shape[2]
+    depth = math.gcd(width, 256)
+    first, second = [], []
+    for start in range(0, width, depth):
+        points = slice(start, start + depth)
+        if split:
+            first.append(contract(potential[:, points], profile[0, :split, points]))
+        second.append(contract(profile[0, split:, points], potential[:, points]))
+    result = functools.reduce(jnp.add, second).T
+    if split:
+        result = jnp.concatenate([functools.reduce(jnp.add, first), result], axis=1)
+    for group in range(groups):
+        staged[group * slabs : (group + 1) * slabs, :] = result[
+            :, group * LANES : (group + 1) * LANES
+        ]
     runs = []
     length = math.gcd(slabs, 4)
     for start in range(0, slabs, length):

time: 20.3 us -> 20.1 us (level)
  no operation moved by 1% of the time
where the time goes in v4:
time: 20.1 us; the launch traced here: 19.9 us
  starting transfers between devices  8.01 us (40%)
  waiting for transfers between devices  4.94 us (25%)
  between operations  3.29 us (16%)
  Pallas kernels  2.73 us (14%)
  other arithmetic  0.62 us (3%)
  local copies, waits for them, and re-layouts  0.33 us (2%)
    ppermute x1, starting transfers between devices, body(): sent = lax.ppermute(sent, 'slab', [(k, k ^ reach) for k in range(count)])  3.1 us
    ppermute x1, starting transfers between devices, body(): other = lax.ppermute(group, 'slab', [(k, k ^ reach) for k in range(count)])  3.09 us
    ppermute x1, starting transfers between devices, body(): arrived.append(lax.ppermute(away[shift - 1], 'valley', pairs))  1.82 us
    ppermute x1, waiting for transfers between devices, body(): other = lax.ppermute(group, 'slab', [(k, k ^ reach) for k in range(count)])  1.81 us
    ppermute x1, waiting for transfers between devices, body(): arrived.append(lax.ppermute(away[shift - 1], 'valley', pairs))  1.19 us
    pallas_call x1, Pallas kernels, body(): pl.pallas_call(project_kernel, out_shape=(jax.ShapeDtypeStruct((slabs + 2...  1.12 us
    ppermute x1, waiting for transfers between devices, body(): sent = lax.ppermute(sent, 'slab', [(k, k ^ reach) for k in range(count)])  0.98 us
    ppermute x2, waiting for transfers between devices, swap(): lax.ppermute(term, 'blk', [(k, (k + shift) % blocks) for k in range(block...  0.97 us
  transfers between devices with their start and end apart: 5, of which 4 were waited for; matrix products, arithmetic and copies ran while one was open for 0% of the time, Pallas kernels for 6%

profile of v4, /device:TPU:0, one launch (start us, length us, event | category | flops | bytes accessed | tf_op | source)
XLA Modules:
  0.0 19.9 jit_solution(1158568895275382570)
XLA Ops:
  0.6 0.0 copy-start.1
  0.6 0.0 copy-start.4
  0.7 0.0 copy-start.5
  0.7 0.0 copy-start.2
  0.7 0.0 copy-start.3
  0.7 0.0 copy-start
  2.6 0.0 copy-done.1
  2.6 0.0 copy-done.4
  2.6 0.0 copy-done.5
  2.6 0.0 copy-done.2
  2.6 0.0 copy-done.3
  2.6 0.3 %copy-done = bf16[1,1024,2048]{2,1,0:T(8,128)(2,1)S(1)} copy-done((bf16[1,1024,2048]{2,1,0:T(8,128)(2,1)S(1)}, bf16[1,1024,2048]{2,1,0:T(8,128)(2,1)}, u32[]{:S(2)}) %copy-start) | copy-done | bytes 4194328
  3.0 1.1 %shard_map.105 = (f32[18,8,128]{2,1,0:T(8,128)S(1)}, f32[4,8,128]{2,1,0:T(8,128)S(1)}, f32[6,8,128]{2,1,0:T(8,128)S(1)}) custom-call(f32[2,8,128]{2,1,0:T(8,128)S(1)} %shard_map.104.level_in, bf16[16,2048]{1,0:T(8,128)(2,1)S(1)} %copy-done.1, f32[1,1024]{1,0:T(1,128)S(1)} %copy-done.4, f32[1,1024]{1,0:T(1,128)S(1)} %copy-done.5, ...), custom_call_target="tpu_custom_call" | custom-call | flops 67108864 | bytes 4194304 | tf_op jit(solution)/shard_map/pallas_call | solution.py:319
  4.1 3.1 %collective-permute-start = (f32[6,8,128]{2,1,0:T(8,128)S(1)}, f32[6,8,128]{2,1,0:T(8,128)S(1)}, u32[]{:S(2)}, u32[]{:S(2)}) collective-permute-start(f32[6,8,128]{2,1,0:T(8,128)S(1)} %get-tuple-element.15.refs_1_), channel_id=1, source_target_pairs={{0,4},{4,0},{8,12},{12,8},{1,5},{5,1},{9,13},{13,9},{2,6},{6,2},{1... | collective-permute-start | bytes 73736 | tf_op jit(solution)/shard_map/ppermute | solution.py:343
  7.2 1.8 %collective-permute-done.refs_2_ = f32[6,8,128]{2,1,0:T(8,128)S(1)} collective-permute-done((f32[6,8,128]{2,1,0:T(8,128)S(1)}, f32[6,8,128]{2,1,0:T(8,128)S(1)}, u32[]{:S(2)}, u32[]{:S(2)}) %collective-permute-start) | collective-permute-done | bytes 24608 | tf_op jit(solution)/shard_map/ppermute | solution.py:343
  9.0 3.1 %collective-permute-start.1 = (f32[2,8,128]{2,1,0:T(8,128)S(1)}, f32[2,8,128]{2,1,0:T(8,128)S(1)}, u32[]{:S(2)}, u32[]{:S(2)}) collective-permute-start(f32[2,8,128]{2,1,0:T(8,128)S(1)} %get-tuple-element.18), channel_id=1, source_target_pairs={{0,8},{4,12},{8,0},{12,4},{1,9},{5,13},{9,1},{13,5},{2,10},{6,14},... | collective-permute-start | bytes 24584 | tf_op jit(solution)/shard_map/ppermute | solution.py:354
  12.8 1.0 %collective-permute-done.1.sent_in = f32[2,8,128]{2,1,0:T(8,128)S(1)} collective-permute-done((f32[2,8,128]{2,1,0:T(8,128)S(1)}, f32[2,8,128]{2,1,0:T(8,128)S(1)}, u32[]{:S(2)}, u32[]{:S(2)}) %collective-permute-start.1) | collective-permute-done | bytes 8224 | tf_op jit(solution)/shard_map/ppermute | solution.py:354
  13.7 0.4 %shard_map.107 = (f32[1,16,1024]{2,1,0:T(8,128)S(1)}, bf16[16,1024]{1,0:T(8,128)(2,1)S(1)}, f32[1,16,512]{2,1,0:T(8,128)S(1)}) custom-call(f32[1]{0:T(128)S(6)} %copy.13.occupation, f32[18,8,128]{2,1,0:T(8,128)S(1)} %get-tuple-element.13.onsite_in, f32[2,8,128]{2,1,0:T(8,128)S(1)} %get-tuple-element.16.outer_in, ...), custom_call_target="tpu_custom_call" | custom-call | flops 16777216 | bytes 1048576 | tf_op jit(solution)/shard_map/pallas_call | solution.py:379
  14.2 0.0 collective-permute-start.2
  14.2 0.3 %shard_map.108.refs_0_ = f32[1,16,512]{2,1,0:T(8,128)S(1)} custom-call(bf16[16,1024]{1,0:T(8,128)(2,1)S(1)} %get-tuple-element.19.half, bf16[1,1024,2048]{2,1,0:T(8,128)(2,1)S(1)} %copy-done), custom_call_target="tpu_custom_call" | custom-call | flops 16777216 | bytes 1048576 | tf_op jit(solution)/shard_map/pallas_call | solution.py:394
  14.4 1.0 %collective-permute-done.2.refs_1_ = f32[1,16,512]{2,1,0:T(8,128)S(1)} collective-permute-done((f32[1,16,512]{2,1,0:T(8,128)S(1)}, f32[1,16,512]{2,1,0:T(8,128)S(1)}, u32[]{:S(2)}, u32[]{:S(2)}) %collective-permute-start.2) | collective-permute-done | bytes 32800 | tf_op jit(solution)/shard_map/ppermute | solution.py:374
  15.4 1.8 %collective-permute-start.4 = (f32[16,512]{1,0:T(8,128)S(1)}, f32[16,512]{1,0:T(8,128)S(1)}, u32[]{:S(2)}, u32[]{:S(2)}) collective-permute-start(f32[16,512]{1,0:T(8,128)S(1)} %shard_map.109.after.rest_0_), channel_id=1, source_target_pairs={{0,2},{2,0},{1,3},{3,1},{4,6},{6,4},{5,7},{7,5},{8,10},{10,8},{9,1... | collective-permute-start | bytes 98312 | tf_op jit(solution)/shard_map/ppermute | solution.py:411
  17.2 0.2 %shard_map.111 = f32[1,16,512]{2,1,0:T(8,128)S(1)} custom-call(bf16[16,1024]{1,0:T(8,128)(2,1)S(1)} %get-tuple-element.19.half, bf16[1,1024,2048]{2,1,0:T(8,128)(2,1)S(1)} %copy-done, f32[16,512]{1,0:T(8,128)S(1)} %shard_map.109.after.rest_0_), custom_call_target="tpu_custom_call" | custom-call | flops 16777216 | bytes 1048576 | tf_op jit(solution)/shard_map/pallas_call | solution.py:394
  17.5 0.0 collective-permute-start.3
  17.5 0.7 %shard_map.110 = (f32[1,16,512]{2,1,0:T(8,128)S(1)}, f32[1,16,1024]{2,1,0:T(8,128)}) custom-call(bf16[16,1024]{1,0:T(8,128)(2,1)S(1)} %get-tuple-element.19.half, bf16[1,1024,2048]{2,1,0:T(8,128)(2,1)S(1)} %copy-done, f32[1,16,1024]{2,1,0:T(8,128)S(1)} %get-tuple-element.20.charge, f32[16,512]{1,0:T(8,128)S(1)} %shard_map.109.after.rest_0_), custom_call_target="tpu_custom_call" | custom-call | flops 16777216 | bytes 1048576 | tf_op jit(solution)/shard_map/pallas_call | solution.py:414
  18.1 1.2 %collective-permute-done.4 = f32[16,512]{1,0:T(8,128)S(1)} collective-permute-done((f32[16,512]{1,0:T(8,128)S(1)}, f32[16,512]{1,0:T(8,128)S(1)}, u32[]{:S(2)}, u32[]{:S(2)}) %collective-permute-start.4) | collective-permute-done | bytes 32800 | tf_op jit(solution)/shard_map/ppermute | solution.py:411
  19.3 0.0 collective-permute-done.3
  19.3 0.6 %bitcast_add_fusion = f32[16,512]{1,0:T(8,128)} fusion(f32[16,512]{1,0:T(8,128)S(1)} %collective-permute-done.4, f32[1,16,512]{2,1,0:T(8,128)S(1)} %get-tuple-element.23, f32[1,16,512]{2,1,0:T(8,128)S(1)} %collective-permute-done.3), kind=kLoop, calls=%fused_computation | loop fusion | flops 16384 | bytes 131072 | tf_op jit(solution)/shard_map/add | solution.py:427
  (3 shorter events, 0.0 us)
Async XLA Ops:
  0.6 2.0 %copy-start.1 = (bf16[16,2048]{1,0:T(8,128)(2,1)S(1)}, bf16[16,2048]{1,0:T(8,128)(2,1)}, u32[]{:S(2)}) copy-start(bf16[16,2048]{1,0:T(8,128)(2,1)} %potential.1) | copy-start | bytes 196612
  0.6 2.0 %copy-start.4 = (f32[1,1024]{1,0:T(1,128)S(1)}, f32[1,1024]{1,0:T(1,128)}, u32[]{:S(2)}) copy-start(f32[1,1024]{1,0:T(1,128)} %mode_energy.1) | copy-start | bytes 12292
  0.7 2.0 %copy-start.5 = (f32[1,1024]{1,0:T(1,128)S(1)}, f32[1,1024]{1,0:T(1,128)}, u32[]{:S(2)}) copy-start(f32[1,1024]{1,0:T(1,128)} %broadening.1) | copy-start | bytes 12292
  0.7 2.0 %copy-start.2 = (f32[1,2,1024]{2,1,0:T(2,128)S(1)}, f32[1,2,1024]{2,1,0:T(2,128)}, u32[]{:S(2)}) copy-start(f32[1,2,1024]{2,1,0:T(2,128)} %self_left.1) | copy-start | bytes 24580
  0.7 2.0 %copy-start.3 = (f32[1,2,1024]{2,1,0:T(2,128)S(1)}, f32[1,2,1024]{2,1,0:T(2,128)}, u32[]{:S(2)}) copy-start(f32[1,2,1024]{2,1,0:T(2,128)} %self_right.1) | copy-start | bytes 24580
  0.7 2.3 %copy-start = (bf16[1,1024,2048]{2,1,0:T(8,128)(2,1)S(1)}, bf16[1,1024,2048]{2,1,0:T(8,128)(2,1)}, u32[]{:S(2)}) copy-start(bf16[1,1024,2048]{2,1,0:T(8,128)(2,1)} %profile.9) | copy-start | bytes 12582916
  4.1 4.9 %collective-permute-start = (f32[6,8,128]{2,1,0:T(8,128)S(1)}, f32[6,8,128]{2,1,0:T(8,128)S(1)}, u32[]{:S(2)}, u32[]{:S(2)}) collective-permute-start(f32[6,8,128]{2,1,0:T(8,128)S(1)} %get-tuple-element.15.refs_1_), channel_id=1, source_target_pairs={{0,4},{4,0},{8,12},{12,8},{1,5},{5,1},{9,13},{13,9},{2,6},{6,2},{1... | collective-permute-start | bytes 73736 | tf_op jit(solution)/shard_map/ppermute | solution.py:343
  9.0 4.7 %collective-permute-start.1 = (f32[2,8,128]{2,1,0:T(8,128)S(1)}, f32[2,8,128]{2,1,0:T(8,128)S(1)}, u32[]{:S(2)}, u32[]{:S(2)}) collective-permute-start(f32[2,8,128]{2,1,0:T(8,128)S(1)} %get-tuple-element.18), channel_id=1, source_target_pairs={{0,8},{4,12},{8,0},{12,4},{1,9},{5,13},{9,1},{13,5},{2,10},{6,14},... | collective-permute-start | bytes 24584 | tf_op jit(solution)/shard_map/ppermute | solution.py:354
  14.2 1.2 %collective-permute-start.2 = (f32[1,16,512]{2,1,0:T(8,128)S(1)}, f32[1,16,512]{2,1,0:T(8,128)S(1)}, u32[]{:S(2)}, u32[]{:S(2)}) collective-permute-start(f32[1,16,512]{2,1,0:T(8,128)S(1)} %get-tuple-element.21), channel_id=1, source_target_pairs={{0,1},{1,0},{2,3},{3,2},{4,5},{5,4},{6,7},{7,6},{8,9},{9,8},{10,11... | collective-permute-start | bytes 98312 | tf_op jit(solution)/shard_map/ppermute | solution.py:374
  15.4 3.9 %collective-permute-start.4 = (f32[16,512]{1,0:T(8,128)S(1)}, f32[16,512]{1,0:T(8,128)S(1)}, u32[]{:S(2)}, u32[]{:S(2)}) collective-permute-start(f32[16,512]{1,0:T(8,128)S(1)} %shard_map.109.after.rest_0_), channel_id=1, source_target_pairs={{0,2},{2,0},{1,3},{3,1},{4,6},{6,4},{5,7},{7,5},{8,10},{10,8},{9,1... | collective-permute-start | bytes 98312 | tf_op jit(solution)/shard_map/ppermute | solution.py:411
  17.5 1.9 %collective-permute-start.3 = (f32[1,16,512]{2,1,0:T(8,128)S(1)}, f32[1,16,512]{2,1,0:T(8,128)S(1)}, u32[]{:S(2)}, u32[]{:S(2)}) collective-permute-start(f32[1,16,512]{2,1,0:T(8,128)S(1)} %shard_map.111), channel_id=1, source_target_pairs={{0,1},{1,0},{2,3},{3,2},{4,5},{5,4},{6,7},{7,6},{8,9},{9,8},{10,11... | collective-permute-start | bytes 98312 | tf_op jit(solution)/shard_map/ppermute | solution.py:374

commit v5 on v4

--- a/solution.py
+++ b/solution.py
@@ -122,22 +122,24 @@
         )
     onsite_out[slabs] = damping
     onsite_out[slabs + 1] = inverse
-    split = groups // 2 * LANES
     width = profile.shape[2]
     depth = math.gcd(width, 256)
-    first, second = [], []
+    block = math.gcd(groups, 2) * LANES
+    totals = [None] * (groups * LANES // block)
     for start in range(0, width, depth):
         points = slice(start, start + depth)
-        if split:
-            first.append(contract(potential[:, points], profile[0, :split, points]))
-        second.append(contract(profile[0, split:, points], potential[:, points]))
-    result = functools.reduce(jnp.add, second).T
-    if split:
-        result = jnp.concatenate([functools.reduce(jnp.add, first), result], axis=1)
-    for group in range(groups):
-        staged[group * slabs : (group + 1) * slabs, :] = result[
-            :, group * LANES : (group + 1) * LANES
-        ]
+        for place, total in enumerate(totals):
+            rows = profile[0, place * block : (place + 1) * block, points]
+            if place % 2:
+                term = contract(rows, potential[:, points])
+            else:
+                term = contract(potential[:, points], rows)
+            totals[place] = term if total is None else total + term
+    for place, total in enumerate(totals):
+        result = total.T if place % 2 else total
+        for column in range(0, block, LANES):
+            group = (place * block + column) // LANES
+            staged[group * slabs : (group + 1) * slabs, :] = result[:, column : column + LANES]
     runs = []
     length = math.gcd(slabs, 4)
     for start in range(0, slabs, length):

time: 20.1 us -> 20 us (level)
  no operation moved by 1% of the time
where the time goes in v5:
time: 20 us; the launch traced here: 19.8 us
  starting transfers between devices  8.01 us (40%)
  waiting for transfers between devices  4.94 us (25%)
  between operations  3.29 us (16%)
  Pallas kernels  2.6 us (13%)
  other arithmetic  0.62 us (3%)
  local copies, waits for them, and re-layouts  0.33 us (2%)
    ppermute x1, starting transfers between devices, body(): sent = lax.ppermute(sent, 'slab', [(k, k ^ reach) for k in range(count)])  3.1 us
    ppermute x1, starting transfers between devices, body(): other = lax.ppermute(group, 'slab', [(k, k ^ reach) for k in range(count)])  3.09 us
    ppermute x1, starting transfers between devices, body(): arrived.append(lax.ppermute(away[shift - 1], 'valley', pairs))  1.82 us
    ppermute x1, waiting for transfers between devices, body(): other = lax.ppermute(group, 'slab', [(k, k ^ reach) for k in range(count)])  1.81 us
    ppermute x1, waiting for transfers between devices, body(): arrived.append(lax.ppermute(away[shift - 1], 'valley', pairs))  1.19 us
    pallas_call x1, Pallas kernels, body(): pl.pallas_call(project_kernel, out_shape=(jax.ShapeDtypeStruct((slabs + 2...  0.98 us
    ppermute x1, waiting for transfers between devices, body(): sent = lax.ppermute(sent, 'slab', [(k, k ^ reach) for k in range(count)])  0.98 us
    ppermute x2, waiting for transfers between devices, swap(): lax.ppermute(term, 'blk', [(k, (k + shift) % blocks) for k in range(block...  0.97 us
  transfers between devices with their start and end apart: 5, of which 4 were waited for; matrix products, arithmetic and copies ran while one was open for 0% of the time, Pallas kernels for 6%

profile of v5, /device:TPU:0, one launch (start us, length us, event | category | flops | bytes accessed | tf_op | source)
XLA Modules:
  0.0 19.8 jit_solution(17640445402459599202)
XLA Ops:
  0.6 0.0 copy-start.1
  0.6 0.0 copy-start.4
  0.7 0.0 copy-start.5
  0.7 0.0 copy-start.2
  0.7 0.0 copy-start.3
  0.7 0.0 copy-start
  2.6 0.0 copy-done.1
  2.6 0.0 copy-done.4
  2.6 0.0 copy-done.5
  2.6 0.0 copy-done.2
  2.6 0.0 copy-done.3
  2.6 0.3 %copy-done = bf16[1,1024,2048]{2,1,0:T(8,128)(2,1)S(1)} copy-done((bf16[1,1024,2048]{2,1,0:T(8,128)(2,1)S(1)}, bf16[1,1024,2048]{2,1,0:T(8,128)(2,1)}, u32[]{:S(2)}) %copy-start) | copy-done | bytes 4194328
  3.0 1.0 %shard_map.105 = (f32[18,8,128]{2,1,0:T(8,128)S(1)}, f32[4,8,128]{2,1,0:T(8,128)S(1)}, f32[6,8,128]{2,1,0:T(8,128)S(1)}) custom-call(f32[2,8,128]{2,1,0:T(8,128)S(1)} %shard_map.104.level_in, bf16[16,2048]{1,0:T(8,128)(2,1)S(1)} %copy-done.1, f32[1,1024]{1,0:T(1,128)S(1)} %copy-done.4, f32[1,1024]{1,0:T(1,128)S(1)} %copy-done.5, ...), custom_call_target="tpu_custom_call" | custom-call | flops 67108864 | bytes 4194304 | tf_op jit(solution)/shard_map/pallas_call | solution.py:321
  3.9 3.1 %collective-permute-start = (f32[6,8,128]{2,1,0:T(8,128)S(1)}, f32[6,8,128]{2,1,0:T(8,128)S(1)}, u32[]{:S(2)}, u32[]{:S(2)}) collective-permute-start(f32[6,8,128]{2,1,0:T(8,128)S(1)} %get-tuple-element.15.refs_1_), channel_id=1, source_target_pairs={{0,4},{4,0},{8,12},{12,8},{1,5},{5,1},{9,13},{13,9},{2,6},{6,2},{1... | collective-permute-start | bytes 73736 | tf_op jit(solution)/shard_map/ppermute | solution.py:345
  7.0 1.8 %collective-permute-done.refs_2_ = f32[6,8,128]{2,1,0:T(8,128)S(1)} collective-permute-done((f32[6,8,128]{2,1,0:T(8,128)S(1)}, f32[6,8,128]{2,1,0:T(8,128)S(1)}, u32[]{:S(2)}, u32[]{:S(2)}) %collective-permute-start) | collective-permute-done | bytes 24608 | tf_op jit(solution)/shard_map/ppermute | solution.py:345
  8.9 3.1 %collective-permute-start.1 = (f32[2,8,128]{2,1,0:T(8,128)S(1)}, f32[2,8,128]{2,1,0:T(8,128)S(1)}, u32[]{:S(2)}, u32[]{:S(2)}) collective-permute-start(f32[2,8,128]{2,1,0:T(8,128)S(1)} %get-tuple-element.18), channel_id=1, source_target_pairs={{0,8},{4,12},{8,0},{12,4},{1,9},{5,13},{9,1},{13,5},{2,10},{6,14},... | collective-permute-start | bytes 24584 | tf_op jit(solution)/shard_map/ppermute | solution.py:356
  12.6 1.0 %collective-permute-done.1.sent_in = f32[2,8,128]{2,1,0:T(8,128)S(1)} collective-permute-done((f32[2,8,128]{2,1,0:T(8,128)S(1)}, f32[2,8,128]{2,1,0:T(8,128)S(1)}, u32[]{:S(2)}, u32[]{:S(2)}) %collective-permute-start.1) | collective-permute-done | bytes 8224 | tf_op jit(solution)/shard_map/ppermute | solution.py:356
  13.6 0.4 %shard_map.107 = (f32[1,16,1024]{2,1,0:T(8,128)S(1)}, bf16[16,1024]{1,0:T(8,128)(2,1)S(1)}, f32[1,16,512]{2,1,0:T(8,128)S(1)}) custom-call(f32[1]{0:T(128)S(6)} %copy.13.occupation, f32[18,8,128]{2,1,0:T(8,128)S(1)} %get-tuple-element.13.onsite_in, f32[2,8,128]{2,1,0:T(8,128)S(1)} %get-tuple-element.16.outer_in, ...), custom_call_target="tpu_custom_call" | custom-call | flops 16777216 | bytes 1048576 | tf_op jit(solution)/shard_map/pallas_call | solution.py:381
  14.0 0.0 collective-permute-start.2
  14.0 0.3 %shard_map.108.refs_0_ = f32[1,16,512]{2,1,0:T(8,128)S(1)} custom-call(bf16[16,1024]{1,0:T(8,128)(2,1)S(1)} %get-tuple-element.19.half, bf16[1,1024,2048]{2,1,0:T(8,128)(2,1)S(1)} %copy-done), custom_call_target="tpu_custom_call" | custom-call | flops 16777216 | bytes 1048576 | tf_op jit(solution)/shard_map/pallas_call | solution.py:396
  14.3 1.0 %collective-permute-done.2.refs_1_ = f32[1,16,512]{2,1,0:T(8,128)S(1)} collective-permute-done((f32[1,16,512]{2,1,0:T(8,128)S(1)}, f32[1,16,512]{2,1,0:T(8,128)S(1)}, u32[]{:S(2)}, u32[]{:S(2)}) %collective-permute-start.2) | collective-permute-done | bytes 32800 | tf_op jit(solution)/shard_map/ppermute | solution.py:376
  15.3 1.8 %collective-permute-start.4 = (f32[16,512]{1,0:T(8,128)S(1)}, f32[16,512]{1,0:T(8,128)S(1)}, u32[]{:S(2)}, u32[]{:S(2)}) collective-permute-start(f32[16,512]{1,0:T(8,128)S(1)} %shard_map.109.after.rest_0_), channel_id=1, source_target_pairs={{0,2},{2,0},{1,3},{3,1},{4,6},{6,4},{5,7},{7,5},{8,10},{10,8},{9,1... | collective-permute-start | bytes 98312 | tf_op jit(solution)/shard_map/ppermute | solution.py:413
  17.1 0.2 %shard_map.111 = f32[1,16,512]{2,1,0:T(8,128)S(1)} custom-call(bf16[16,1024]{1,0:T(8,128)(2,1)S(1)} %get-tuple-element.19.half, bf16[1,1024,2048]{2,1,0:T(8,128)(2,1)S(1)} %copy-done, f32[16,512]{1,0:T(8,128)S(1)} %shard_map.109.after.rest_0_), custom_call_target="tpu_custom_call" | custom-call | flops 16777216 | bytes 1048576 | tf_op jit(solution)/shard_map/pallas_call | solution.py:396
  17.3 0.0 collective-permute-start.3
  17.3 0.7 %shard_map.110 = (f32[1,16,512]{2,1,0:T(8,128)S(1)}, f32[1,16,1024]{2,1,0:T(8,128)}) custom-call(bf16[16,1024]{1,0:T(8,128)(2,1)S(1)} %get-tuple-element.19.half, bf16[1,1024,2048]{2,1,0:T(8,128)(2,1)S(1)} %copy-done, f32[1,16,1024]{2,1,0:T(8,128)S(1)} %get-tuple-element.20.charge, f32[16,512]{1,0:T(8,128)S(1)} %shard_map.109.after.rest_0_), custom_call_target="tpu_custom_call" | custom-call | flops 16777216 | bytes 1048576 | tf_op jit(solution)/shard_map/pallas_call | solution.py:416
  18.0 1.2 %collective-permute-done.4 = f32[16,512]{1,0:T(8,128)S(1)} collective-permute-done((f32[16,512]{1,0:T(8,128)S(1)}, f32[16,512]{1,0:T(8,128)S(1)}, u32[]{:S(2)}, u32[]{:S(2)}) %collective-permute-start.4) | collective-permute-done | bytes 32800 | tf_op jit(solution)/shard_map/ppermute | solution.py:413
  19.2 0.0 collective-permute-done.3
  19.2 0.6 %bitcast_add_fusion = f32[16,512]{1,0:T(8,128)} fusion(f32[16,512]{1,0:T(8,128)S(1)} %collective-permute-done.4, f32[1,16,512]{2,1,0:T(8,128)S(1)} %get-tuple-element.23, f32[1,16,512]{2,1,0:T(8,128)S(1)} %collective-permute-done.3), kind=kLoop, calls=%fused_computation | loop fusion | flops 16384 | bytes 131072 | tf_op jit(solution)/shard_map/add | solution.py:429
  (3 shorter events, 0.0 us)
Async XLA Ops:
  0.6 2.0 %copy-start.1 = (bf16[16,2048]{1,0:T(8,128)(2,1)S(1)}, bf16[16,2048]{1,0:T(8,128)(2,1)}, u32[]{:S(2)}) copy-start(bf16[16,2048]{1,0:T(8,128)(2,1)} %potential.1) | copy-start | bytes 196612
  0.6 2.0 %copy-start.4 = (f32[1,1024]{1,0:T(1,128)S(1)}, f32[1,1024]{1,0:T(1,128)}, u32[]{:S(2)}) copy-start(f32[1,1024]{1,0:T(1,128)} %mode_energy.1) | copy-start | bytes 12292
  0.7 2.0 %copy-start.5 = (f32[1,1024]{1,0:T(1,128)S(1)}, f32[1,1024]{1,0:T(1,128)}, u32[]{:S(2)}) copy-start(f32[1,1024]{1,0:T(1,128)} %broadening.1) | copy-start | bytes 12292
  0.7 2.0 %copy-start.2 = (f32[1,2,1024]{2,1,0:T(2,128)S(1)}, f32[1,2,1024]{2,1,0:T(2,128)}, u32[]{:S(2)}) copy-start(f32[1,2,1024]{2,1,0:T(2,128)} %self_left.1) | copy-start | bytes 24580
  0.7 2.0 %copy-start.3 = (f32[1,2,1024]{2,1,0:T(2,128)S(1)}, f32[1,2,1024]{2,1,0:T(2,128)}, u32[]{:S(2)}) copy-start(f32[1,2,1024]{2,1,0:T(2,128)} %self_right.1) | copy-start | bytes 24580
  0.7 2.3 %copy-start = (bf16[1,1024,2048]{2,1,0:T(8,128)(2,1)S(1)}, bf16[1,1024,2048]{2,1,0:T(8,128)(2,1)}, u32[]{:S(2)}) copy-start(bf16[1,1024,2048]{2,1,0:T(8,128)(2,1)} %profile.9) | copy-start | bytes 12582916
  3.9 4.9 %collective-permute-start = (f32[6,8,128]{2,1,0:T(8,128)S(1)}, f32[6,8,128]{2,1,0:T(8,128)S(1)}, u32[]{:S(2)}, u32[]{:S(2)}) collective-permute-start(f32[6,8,128]{2,1,0:T(8,128)S(1)} %get-tuple-element.15.refs_1_), channel_id=1, source_target_pairs={{0,4},{4,0},{8,12},{12,8},{1,5},{5,1},{9,13},{13,9},{2,6},{6,2},{1... | collective-permute-start | bytes 73736 | tf_op jit(solution)/shard_map/ppermute | solution.py:345
  8.9 4.7 %collective-permute-start.1 = (f32[2,8,128]{2,1,0:T(8,128)S(1)}, f32[2,8,128]{2,1,0:T(8,128)S(1)}, u32[]{:S(2)}, u32[]{:S(2)}) collective-permute-start(f32[2,8,128]{2,1,0:T(8,128)S(1)} %get-tuple-element.18), channel_id=1, source_target_pairs={{0,8},{4,12},{8,0},{12,4},{1,9},{5,13},{9,1},{13,5},{2,10},{6,14},... | collective-permute-start | bytes 24584 | tf_op jit(solution)/shard_map/ppermute | solution.py:356
  14.0 1.2 %collective-permute-start.2 = (f32[1,16,512]{2,1,0:T(8,128)S(1)}, f32[1,16,512]{2,1,0:T(8,128)S(1)}, u32[]{:S(2)}, u32[]{:S(2)}) collective-permute-start(f32[1,16,512]{2,1,0:T(8,128)S(1)} %get-tuple-element.21), channel_id=1, source_target_pairs={{0,1},{1,0},{2,3},{3,2},{4,5},{5,4},{6,7},{7,6},{8,9},{9,8},{10,11... | collective-permute-start | bytes 98312 | tf_op jit(solution)/shard_map/ppermute | solution.py:376
  15.3 3.9 %collective-permute-start.4 = (f32[16,512]{1,0:T(8,128)S(1)}, f32[16,512]{1,0:T(8,128)S(1)}, u32[]{:S(2)}, u32[]{:S(2)}) collective-permute-start(f32[16,512]{1,0:T(8,128)S(1)} %shard_map.109.after.rest_0_), channel_id=1, source_target_pairs={{0,2},{2,0},{1,3},{3,1},{4,6},{6,4},{5,7},{7,5},{8,10},{10,8},{9,1... | collective-permute-start | bytes 98312 | tf_op jit(solution)/shard_map/ppermute | solution.py:413
  17.3 1.9 %collective-permute-start.3 = (f32[1,16,512]{2,1,0:T(8,128)S(1)}, f32[1,16,512]{2,1,0:T(8,128)S(1)}, u32[]{:S(2)}, u32[]{:S(2)}) collective-permute-start(f32[1,16,512]{2,1,0:T(8,128)S(1)} %shard_map.111), channel_id=1, source_target_pairs={{0,1},{1,0},{2,3},{3,2},{4,5},{5,4},{6,7},{7,6},{8,9},{9,8},{10,11... | collective-permute-start | bytes 98312 | tf_op jit(solution)/shard_map/ppermute | solution.py:376

commit v6 on v5

--- a/solution.py
+++ b/solution.py
@@ -266,13 +266,6 @@
     return close(2 * reach, contact, *widen(reach, *runs))
 
 
-def add_blocks(mine, *arrived):
-    total = mine
-    for part in arrived:
-        total = total + part
-    return tuple(total[place] for place in range(mine.shape[0]))
-
-
 def on_vmem(function, *arrays):
     def kernel(*refs):
         results = function(*(ref[...] for ref in refs[: len(arrays)]))
@@ -365,8 +358,8 @@
     def term_shapes(plan, count):
         return [jax.ShapeDtypeStruct((len(plan[2]), slabs, piece), f32)] * count
 
-    def cost(plan, count):
-        columns = len(plan[2]) * count * piece
+    def cost(plan, count, scale=1):
+        columns = len(plan[2]) * count * piece // scale
         return pl.CostEstimate(
             flops=2 * slabs * columns * modes, bytes_accessed=2 * columns * modes, transcendentals=0
         )
@@ -399,20 +392,30 @@
             in_specs=[vmem] * 2 + [anywhere] * len(after),
             out_specs=[vmem] * len(block_shifts),
             compiler_params=pltpu.CompilerParams(vmem_limit_bytes=VMEM_LIMIT),
-            cost_estimate=cost(plan, len(block_shifts)),
+            cost_estimate=cost(plan, len(block_shifts), 512),
         )(half, mode_density, *after)
 
-    others = swap(others)
+    def send(terms, block_shift):
+        received = []
+        for shift in range(1, valleys):
+            pairs = [
+                (v * blocks + b, (v + shift) % valleys * blocks + (b + block_shift) % blocks)
+                for v in range(valleys)
+                for b in range(blocks)
+            ]
+            received.append(lax.ppermute(terms[shift - 1], ("valley", "blk"), pairs))
+        return received
+
     arrived = []
     after = half
     if valleys > 1:
-        away = on_vmem(add_blocks, *terms_of(away_plan, (0,)), *others)
-        after = away[0]
-        for shift in range(1, valleys):
-            pairs = [(k, (k + shift) % valleys) for k in range(valleys)]
-            arrived.append(lax.ppermute(away[shift - 1], "valley", pairs))
-        if blocks > 1:
-            others = swap(terms_of(home_plan, range(1, blocks), after))
+        straight = terms_of(away_plan, (0,))[0]
+        arrived += send(straight, 0)
+        for block_shift, term in enumerate(others, 1):
+            arrived += send(term, block_shift)
+        after = straight
+        others = terms_of(home_plan, range(1, blocks), after) if blocks > 1 else []
+    others = swap(others)
     term, charge = pl.pallas_call(
         functools.partial(store_kernel, home_plan),
         out_shape=term_shapes(home_plan, 1) + [jax.ShapeDtypeStruct(charge.shape, f32)],
@@ -420,7 +423,7 @@
         out_specs=[vmem, anywhere],
         scratch_shapes=[pltpu.SemaphoreType.DMA],
         compiler_params=pltpu.CompilerParams(vmem_limit_bytes=VMEM_LIMIT),
-        cost_estimate=cost(home_plan, 1),
+        cost_estimate=cost(home_plan, 1, 512),
     )(half, mode_density, charge, after)
     density = term[0]
     for part in others:

time: 20 us -> 19.4 us (0.970); the launches traced: 19.8 us -> 19 us
  waiting for transfers between devices: 4.94 us -> 4.01 us
    ppermute x2 -> x1, waiting for transfers between devices: 0.97 us -> 0.01 us  [swap(): lax.ppermute(term, 'blk', [(k, (k + shift) % blocks) for k in range(block...]
    ppermute x1 -> x2, starting transfers between devices: 1.82 us -> 1.88 us  [send(): received.append(lax.ppermute(terms[shift - 1], ('valley', 'blk'), pairs))]
    ppermute x1 -> x2, waiting for transfers between devices: 1.19 us -> 1.22 us  [send(): received.append(lax.ppermute(terms[shift - 1], ('valley', 'blk'), pairs))]
  transfers between devices with their start and end apart: 5 -> 5, of which waited for: 4 -> 4; matrix products, arithmetic and copies ran while one was open for 0% -> 0% of each run, Pallas kernels for 6% -> 5%
where the time goes in v6:
time: 19.4 us; the launch traced here: 19 us
  starting transfers between devices  8.15 us (42%)
  waiting for transfers between devices  4.01 us (21%)
  between operations  3.29 us (17%)
  Pallas kernels  2.58 us (13%)
  other arithmetic  0.63 us (3%)
  local copies, waits for them, and re-layouts  0.33 us (2%)
    ppermute x1, starting transfers between devices, body(): sent = lax.ppermute(sent, 'slab', [(k, k ^ reach) for k in range(count)])  3.1 us
    ppermute x1, starting transfers between devices, body(): other = lax.ppermute(group, 'slab', [(k, k ^ reach) for k in range(count)])  3.09 us
    ppermute x2, starting transfers between devices, send(): received.append(lax.ppermute(terms[shift - 1], ('valley', 'blk'), pairs))  1.88 us
    ppermute x1, waiting for transfers between devices, body(): other = lax.ppermute(group, 'slab', [(k, k ^ reach) for k in range(count)])  1.81 us
    ppermute x2, waiting for transfers between devices, send(): received.append(lax.ppermute(terms[shift - 1], ('valley', 'blk'), pairs))  1.22 us
    pallas_call x1, Pallas kernels, body(): pl.pallas_call(project_kernel, out_shape=(jax.ShapeDtypeStruct((slabs + 2...  0.98 us
    ppermute x1, waiting for transfers between devices, body(): sent = lax.ppermute(sent, 'slab', [(k, k ^ reach) for k in range(count)])  0.98 us
    pallas_call x1, Pallas kernels, body(): pl.pallas_call(functools.partial(store_kernel, home_plan), out_shape=term...  0.64 us
  transfers between devices with their start and end apart: 5, of which 4 were waited for; matrix products, arithmetic and copies ran while one was open for 0% of the time, Pallas kernels for 5%

profile of v6, /device:TPU:0, one launch (start us, length us, event | category | flops | bytes accessed | tf_op | source)
XLA Modules:
  0.0 19.0 jit_solution(6697804766959852850)
XLA Ops:
  0.6 0.0 copy-start.1
  0.6 0.0 copy-start.4
  0.7 0.0 copy-start.5
  0.7 0.0 copy-start.2
  0.7 0.0 copy-start.3
  0.7 0.0 copy-start
  2.6 0.0 copy-done.1
  2.6 0.0 copy-done.4
  2.6 0.0 copy-done.5
  2.6 0.0 copy-done.2
  2.6 0.0 copy-done.3
  2.6 0.3 %copy-done = bf16[1,1024,2048]{2,1,0:T(8,128)(2,1)S(1)} copy-done((bf16[1,1024,2048]{2,1,0:T(8,128)(2,1)S(1)}, bf16[1,1024,2048]{2,1,0:T(8,128)(2,1)}, u32[]{:S(2)}) %copy-start) | copy-done | bytes 4194328
  3.0 1.0 %shard_map.105 = (f32[18,8,128]{2,1,0:T(8,128)S(1)}, f32[4,8,128]{2,1,0:T(8,128)S(1)}, f32[6,8,128]{2,1,0:T(8,128)S(1)}) custom-call(f32[2,8,128]{2,1,0:T(8,128)S(1)} %shard_map.104.level_in, bf16[16,2048]{1,0:T(8,128)(2,1)S(1)} %copy-done.1, f32[1,1024]{1,0:T(1,128)S(1)} %copy-done.4, f32[1,1024]{1,0:T(1,128)S(1)} %copy-done.5, ...), custom_call_target="tpu_custom_call" | custom-call | flops 67108864 | bytes 4194304 | tf_op jit(solution)/shard_map/pallas_call | solution.py:314
  3.9 3.1 %collective-permute-start = (f32[6,8,128]{2,1,0:T(8,128)S(1)}, f32[6,8,128]{2,1,0:T(8,128)S(1)}, u32[]{:S(2)}, u32[]{:S(2)}) collective-permute-start(f32[6,8,128]{2,1,0:T(8,128)S(1)} %get-tuple-element.15.refs_1_), channel_id=1, source_target_pairs={{0,4},{4,0},{8,12},{12,8},{1,5},{5,1},{9,13},{13,9},{2,6},{6,2},{1... | collective-permute-start | bytes 73736 | tf_op jit(solution)/shard_map/ppermute | solution.py:338
  7.0 1.8 %collective-permute-done.refs_2_ = f32[6,8,128]{2,1,0:T(8,128)S(1)} collective-permute-done((f32[6,8,128]{2,1,0:T(8,128)S(1)}, f32[6,8,128]{2,1,0:T(8,128)S(1)}, u32[]{:S(2)}, u32[]{:S(2)}) %collective-permute-start) | collective-permute-done | bytes 24608 | tf_op jit(solution)/shard_map/ppermute | solution.py:338
  8.9 3.1 %collective-permute-start.1 = (f32[2,8,128]{2,1,0:T(8,128)S(1)}, f32[2,8,128]{2,1,0:T(8,128)S(1)}, u32[]{:S(2)}, u32[]{:S(2)}) collective-permute-start(f32[2,8,128]{2,1,0:T(8,128)S(1)} %get-tuple-element.18), channel_id=1, source_target_pairs={{0,8},{4,12},{8,0},{12,4},{1,9},{5,13},{9,1},{13,5},{2,10},{6,14},... | collective-permute-start | bytes 24584 | tf_op jit(solution)/shard_map/ppermute | solution.py:349
  12.6 1.0 %collective-permute-done.1.sent_in = f32[2,8,128]{2,1,0:T(8,128)S(1)} collective-permute-done((f32[2,8,128]{2,1,0:T(8,128)S(1)}, f32[2,8,128]{2,1,0:T(8,128)S(1)}, u32[]{:S(2)}, u32[]{:S(2)}) %collective-permute-start.1) | collective-permute-done | bytes 8224 | tf_op jit(solution)/shard_map/ppermute | solution.py:349
  13.6 0.4 %shard_map.107 = (f32[1,16,1024]{2,1,0:T(8,128)S(1)}, bf16[16,1024]{1,0:T(8,128)(2,1)S(1)}, f32[1,16,512]{2,1,0:T(8,128)S(1)}) custom-call(f32[1]{0:T(128)S(6)} %copy.13.occupation, f32[18,8,128]{2,1,0:T(8,128)S(1)} %get-tuple-element.13.onsite_in, f32[2,8,128]{2,1,0:T(8,128)S(1)} %get-tuple-element.16.outer_in, ...), custom_call_target="tpu_custom_call" | custom-call | flops 16777216 | bytes 1048576 | tf_op jit(solution)/shard_map/pallas_call | solution.py:374
  14.0 0.3 %shard_map.108.after.rest_0_ = f32[1,16,512]{2,1,0:T(8,128)S(1)} custom-call(bf16[16,1024]{1,0:T(8,128)(2,1)S(1)} %get-tuple-element.19.half, bf16[1,1024,2048]{2,1,0:T(8,128)(2,1)S(1)} %copy-done), custom_call_target="tpu_custom_call" | custom-call | flops 32768 | bytes 2048 | tf_op jit(solution)/shard_map/pallas_call | solution.py:389
  14.3 0.0 collective-permute-start.4
  14.3 1.9 %collective-permute-start.3 = (f32[16,512]{1,0:T(8,128)S(1)}, f32[16,512]{1,0:T(8,128)S(1)}, u32[]{:S(2)}, u32[]{:S(2)}) collective-permute-start(f32[16,512]{1,0:T(8,128)S(1)} %bitcast.6), channel_id=1, source_target_pairs={{0,2},{1,3},{2,0},{3,1},{4,6},{5,7},{6,4},{7,5},{8,10},{9,11},{10,... | collective-permute-start | bytes 98312 | tf_op jit(solution)/shard_map/ppermute | solution.py:406
  16.2 0.2 %shard_map.110 = f32[1,16,512]{2,1,0:T(8,128)S(1)} custom-call(bf16[16,1024]{1,0:T(8,128)(2,1)S(1)} %get-tuple-element.19.half, bf16[1,1024,2048]{2,1,0:T(8,128)(2,1)S(1)} %copy-done, f32[1,16,512]{2,1,0:T(8,128)S(1)} %shard_map.108.after.rest_0_), custom_call_target="tpu_custom_call" | custom-call | flops 32768 | bytes 2048 | tf_op jit(solution)/shard_map/pallas_call | solution.py:389
  16.4 0.1 collective-permute-start.2
  16.5 0.6 %shard_map.109 = (f32[1,16,512]{2,1,0:T(8,128)S(1)}, f32[1,16,1024]{2,1,0:T(8,128)}) custom-call(bf16[16,1024]{1,0:T(8,128)(2,1)S(1)} %get-tuple-element.19.half, bf16[1,1024,2048]{2,1,0:T(8,128)(2,1)S(1)} %copy-done, f32[1,16,1024]{2,1,0:T(8,128)S(1)} %get-tuple-element.20.charge, f32[1,16,512]{2,1,0:T(8,128)S(1)} %shard_map.108.after.rest_0_), custom_call_target="tpu_custom_call" | custom-call | flops 32768 | bytes 2048 | tf_op jit(solution)/shard_map/pallas_call | solution.py:419
  17.1 0.5 %collective-permute-done.4 = f32[16,512]{1,0:T(8,128)S(1)} collective-permute-done((f32[16,512]{1,0:T(8,128)S(1)}, f32[16,512]{1,0:T(8,128)S(1)}, u32[]{:S(2)}, u32[]{:S(2)}) %collective-permute-start.4) | collective-permute-done | bytes 32800 | tf_op jit(solution)/shard_map/ppermute | solution.py:406
  17.6 0.7 %collective-permute-done.3 = f32[16,512]{1,0:T(8,128)S(1)} collective-permute-done((f32[16,512]{1,0:T(8,128)S(1)}, f32[16,512]{1,0:T(8,128)S(1)}, u32[]{:S(2)}, u32[]{:S(2)}) %collective-permute-start.3) | collective-permute-done | bytes 32800 | tf_op jit(solution)/shard_map/ppermute | solution.py:406
  18.4 0.0 collective-permute-done.2
  18.4 0.6 %fusion = f32[16,512]{1,0:T(8,128)} fusion(f32[16,512]{1,0:T(8,128)S(1)} %collective-permute-done.4, f32[16,512]{1,0:T(8,128)S(1)} %collective-permute-done.3, f32[1,16,512]{2,1,0:T(8,128)S(1)} %get-tuple-element.22, f32[1,16,512]{2,1,0:T(8,128)S(1)} %collective-permute-done.2), kind=kLoop, calls=%fused_computation.1 | loop fusion | flops 24576 | bytes 163840 | tf_op jit(solution)/shard_map/add | solution.py:432
  (2 shorter events, 0.0 us)
Async XLA Ops:
  0.6 2.0 %copy-start.1 = (bf16[16,2048]{1,0:T(8,128)(2,1)S(1)}, bf16[16,2048]{1,0:T(8,128)(2,1)}, u32[]{:S(2)}) copy-start(bf16[16,2048]{1,0:T(8,128)(2,1)} %potential.1) | copy-start | bytes 196612
  0.6 2.0 %copy-start.4 = (f32[1,1024]{1,0:T(1,128)S(1)}, f32[1,1024]{1,0:T(1,128)}, u32[]{:S(2)}) copy-start(f32[1,1024]{1,0:T(1,128)} %mode_energy.1) | copy-start | bytes 12292
  0.7 2.0 %copy-start.5 = (f32[1,1024]{1,0:T(1,128)S(1)}, f32[1,1024]{1,0:T(1,128)}, u32[]{:S(2)}) copy-start(f32[1,1024]{1,0:T(1,128)} %broadening.1) | copy-start | bytes 12292
  0.7 2.0 %copy-start.2 = (f32[1,2,1024]{2,1,0:T(2,128)S(1)}, f32[1,2,1024]{2,1,0:T(2,128)}, u32[]{:S(2)}) copy-start(f32[1,2,1024]{2,1,0:T(2,128)} %self_left.1) | copy-start | bytes 24580
  0.7 2.0 %copy-start.3 = (f32[1,2,1024]{2,1,0:T(2,128)S(1)}, f32[1,2,1024]{2,1,0:T(2,128)}, u32[]{:S(2)}) copy-start(f32[1,2,1024]{2,1,0:T(2,128)} %self_right.1) | copy-start | bytes 24580
  0.7 2.3 %copy-start = (bf16[1,1024,2048]{2,1,0:T(8,128)(2,1)S(1)}, bf16[1,1024,2048]{2,1,0:T(8,128)(2,1)}, u32[]{:S(2)}) copy-start(bf16[1,1024,2048]{2,1,0:T(8,128)(2,1)} %profile.9) | copy-start | bytes 12582916
  3.9 4.9 %collective-permute-start = (f32[6,8,128]{2,1,0:T(8,128)S(1)}, f32[6,8,128]{2,1,0:T(8,128)S(1)}, u32[]{:S(2)}, u32[]{:S(2)}) collective-permute-start(f32[6,8,128]{2,1,0:T(8,128)S(1)} %get-tuple-element.15.refs_1_), channel_id=1, source_target_pairs={{0,4},{4,0},{8,12},{12,8},{1,5},{5,1},{9,13},{13,9},{2,6},{6,2},{1... | collective-permute-start | bytes 73736 | tf_op jit(solution)/shard_map/ppermute | solution.py:338
  8.9 4.7 %collective-permute-start.1 = (f32[2,8,128]{2,1,0:T(8,128)S(1)}, f32[2,8,128]{2,1,0:T(8,128)S(1)}, u32[]{:S(2)}, u32[]{:S(2)}) collective-permute-start(f32[2,8,128]{2,1,0:T(8,128)S(1)} %get-tuple-element.18), channel_id=1, source_target_pairs={{0,8},{4,12},{8,0},{12,4},{1,9},{5,13},{9,1},{13,5},{2,10},{6,14},... | collective-permute-start | bytes 24584 | tf_op jit(solution)/shard_map/ppermute | solution.py:349
  14.3 3.4 %collective-permute-start.4 = (f32[16,512]{1,0:T(8,128)S(1)}, f32[16,512]{1,0:T(8,128)S(1)}, u32[]{:S(2)}, u32[]{:S(2)}) collective-permute-start(f32[16,512]{1,0:T(8,128)S(1)} %bitcast.7), channel_id=1, source_target_pairs={{0,3},{1,2},{2,1},{3,0},{4,7},{5,6},{6,5},{7,4},{8,11},{9,10},{10,... | collective-permute-start | bytes 98312 | tf_op jit(solution)/shard_map/ppermute | solution.py:406
  14.3 4.1 %collective-permute-start.3 = (f32[16,512]{1,0:T(8,128)S(1)}, f32[16,512]{1,0:T(8,128)S(1)}, u32[]{:S(2)}, u32[]{:S(2)}) collective-permute-start(f32[16,512]{1,0:T(8,128)S(1)} %bitcast.6), channel_id=1, source_target_pairs={{0,2},{1,3},{2,0},{3,1},{4,6},{5,7},{6,4},{7,5},{8,10},{9,11},{10,... | collective-permute-start | bytes 98312 | tf_op jit(solution)/shard_map/ppermute | solution.py:406
  16.4 2.0 %collective-permute-start.2 = (f32[1,16,512]{2,1,0:T(8,128)S(1)}, f32[1,16,512]{2,1,0:T(8,128)S(1)}, u32[]{:S(2)}, u32[]{:S(2)}) collective-permute-start(f32[1,16,512]{2,1,0:T(8,128)S(1)} %shard_map.110), channel_id=1, source_target_pairs={{0,1},{1,0},{2,3},{3,2},{4,5},{5,4},{6,7},{7,6},{8,9},{9,8},{10,11... | collective-permute-start | bytes 98312 | tf_op jit(solution)/shard_map/ppermute | solution.py:369

commit v7 on v6

--- a/solution.py
+++ b/solution.py
@@ -175,6 +175,7 @@
 def charge_kernel(
     reach,
     plan,
+    block_shifts,
     occupation,
     onsite_in,
     outer_in,
@@ -211,7 +212,7 @@
         rows = staged[group * slabs : (group + 1) * slabs, :]
         charge[0, :, columns] = rows
         half[:, columns] = rows.astype(jnp.bfloat16)
-    for term, block_shift in zip(terms, range(1, plan[1]), strict=True):
+    for term, block_shift in zip(terms, block_shifts, strict=True):
         multiply(half, profile, term, *plan, block_shift)
 
 
@@ -371,18 +372,19 @@
         ]
 
     first_plan = away_plan if valleys > 1 else home_plan
+    first_shifts = [*range(1, blocks)] + [0] * (valleys > 1)
     charge, half, *others = pl.pallas_call(
-        functools.partial(charge_kernel, reach, first_plan),
+        functools.partial(charge_kernel, reach, first_plan, first_shifts),
         out_shape=[
             jax.ShapeDtypeStruct((1, slabs, modes), f32),
             jax.ShapeDtypeStruct((slabs, modes), jnp.bfloat16),
         ]
-        + term_shapes(first_plan, blocks - 1),
+        + term_shapes(first_plan, len(first_shifts)),
         in_specs=[smem] + [vmem] * 5,
-        out_specs=[vmem] * (blocks + 1),
+        out_specs=[vmem] * (2 + len(first_shifts)),
         scratch_shapes=[pltpu.VMEM((groups * slabs, LANES), f32)],
         compiler_params=pltpu.CompilerParams(vmem_limit_bytes=VMEM_LIMIT),
-        cost_estimate=cost(first_plan, blocks - 1),
+        cost_estimate=cost(first_plan, len(first_shifts)),
     )(occupation, onsite, outer, inner_run, sent, mode_density)
 
     def terms_of(plan, block_shifts, *after):
@@ -409,11 +411,9 @@
     arrived = []
     after = half
     if valleys > 1:
-        straight = terms_of(away_plan, (0,))[0]
-        arrived += send(straight, 0)
-        for block_shift, term in enumerate(others, 1):
+        for block_shift, term in reversed([*zip(first_shifts, others, strict=True)]):
             arrived += send(term, block_shift)
-        after = straight
+        after = others[-1]
         others = terms_of(home_plan, range(1, blocks), after) if blocks > 1 else []
     others = swap(others)
     term, charge = pl.pallas_call(

time: 19.4 us -> 19.2 us (0.990)
    pallas_call x2 -> x1, Pallas kernels: 0.5 us -> 0.24 us  [terms_of(): pl.pallas_call(functools.partial(term_kernel, plan, block_shifts), out_sh...]
where the time goes in v7:
time: 19.2 us; the launch traced here: 18.9 us
  starting transfers between devices  8.16 us (42%)
  waiting for transfers between devices  4.01 us (21%)
  between operations  3.29 us (17%)
  Pallas kernels  2.46 us (13%)
  other arithmetic  0.63 us (3%)
  local copies, waits for them, and re-layouts  0.33 us (2%)
    ppermute x1, starting transfers between devices, body(): sent = lax.ppermute(sent, 'slab', [(k, k ^ reach) for k in range(count)])  3.1 us
    ppermute x1, starting transfers between devices, body(): other = lax.ppermute(group, 'slab', [(k, k ^ reach) for k in range(count)])  3.09 us
    ppermute x2, starting transfers between devices, send(): received.append(lax.ppermute(terms[shift - 1], ('valley', 'blk'), pairs))  1.88 us
    ppermute x1, waiting for transfers between devices, body(): other = lax.ppermute(group, 'slab', [(k, k ^ reach) for k in range(count)])  1.81 us
    ppermute x2, waiting for transfers between devices, send(): received.append(lax.ppermute(terms[shift - 1], ('valley', 'blk'), pairs))  1.22 us
    pallas_call x1, Pallas kernels, body(): pl.pallas_call(project_kernel, out_shape=(jax.ShapeDtypeStruct((slabs + 2...  0.98 us
    ppermute x1, waiting for transfers between devices, body(): sent = lax.ppermute(sent, 'slab', [(k, k ^ reach) for k in range(count)])  0.98 us
    pallas_call x1, Pallas kernels, body(): pl.pallas_call(functools.partial(store_kernel, home_plan), out_shape=term...  0.64 us
  transfers between devices with their start and end apart: 5, of which 4 were waited for; matrix products, arithmetic and copies ran while one was open for 0% of the time, Pallas kernels for 5%

profile of v7, /device:TPU:0, one launch (start us, length us, event | category | flops | bytes accessed | tf_op | source)
XLA Modules:
  0.0 18.9 jit_solution(14292702559661137089)
XLA Ops:
  0.6 0.0 copy-start.1
  0.6 0.0 copy-start.4
  0.7 0.0 copy-start.5
  0.7 0.0 copy-start.2
  0.7 0.0 copy-start.3
  0.7 0.0 copy-start
  2.6 0.0 copy-done.1
  2.6 0.0 copy-done.4
  2.6 0.0 copy-done.5
  2.6 0.0 copy-done.2
  2.6 0.0 copy-done.3
  2.6 0.3 %copy-done = bf16[1,1024,2048]{2,1,0:T(8,128)(2,1)S(1)} copy-done((bf16[1,1024,2048]{2,1,0:T(8,128)(2,1)S(1)}, bf16[1,1024,2048]{2,1,0:T(8,128)(2,1)}, u32[]{:S(2)}) %copy-start) | copy-done | bytes 4194328
  3.0 1.0 %shard_map.105 = (f32[18,8,128]{2,1,0:T(8,128)S(1)}, f32[4,8,128]{2,1,0:T(8,128)S(1)}, f32[6,8,128]{2,1,0:T(8,128)S(1)}) custom-call(f32[2,8,128]{2,1,0:T(8,128)S(1)} %shard_map.104.level_in, bf16[16,2048]{1,0:T(8,128)(2,1)S(1)} %copy-done.1, f32[1,1024]{1,0:T(1,128)S(1)} %copy-done.4, f32[1,1024]{1,0:T(1,128)S(1)} %copy-done.5, ...), custom_call_target="tpu_custom_call" | custom-call | flops 67108864 | bytes 4194304 | tf_op jit(solution)/shard_map/pallas_call | solution.py:315
  3.9 3.1 %collective-permute-start = (f32[6,8,128]{2,1,0:T(8,128)S(1)}, f32[6,8,128]{2,1,0:T(8,128)S(1)}, u32[]{:S(2)}, u32[]{:S(2)}) collective-permute-start(f32[6,8,128]{2,1,0:T(8,128)S(1)} %get-tuple-element.16.refs_1_), channel_id=1, source_target_pairs={{0,4},{4,0},{8,12},{12,8},{1,5},{5,1},{9,13},{13,9},{2,6},{6,2},{1... | collective-permute-start | bytes 73736 | tf_op jit(solution)/shard_map/ppermute | solution.py:339
  7.0 1.8 %collective-permute-done.refs_2_ = f32[6,8,128]{2,1,0:T(8,128)S(1)} collective-permute-done((f32[6,8,128]{2,1,0:T(8,128)S(1)}, f32[6,8,128]{2,1,0:T(8,128)S(1)}, u32[]{:S(2)}, u32[]{:S(2)}) %collective-permute-start) | collective-permute-done | bytes 24608 | tf_op jit(solution)/shard_map/ppermute | solution.py:339
  8.9 3.1 %collective-permute-start.1 = (f32[2,8,128]{2,1,0:T(8,128)S(1)}, f32[2,8,128]{2,1,0:T(8,128)S(1)}, u32[]{:S(2)}, u32[]{:S(2)}) collective-permute-start(f32[2,8,128]{2,1,0:T(8,128)S(1)} %get-tuple-element.19), channel_id=1, source_target_pairs={{0,8},{4,12},{8,0},{12,4},{1,9},{5,13},{9,1},{13,5},{2,10},{6,14},... | collective-permute-start | bytes 24584 | tf_op jit(solution)/shard_map/ppermute | solution.py:350
  12.6 1.0 %collective-permute-done.1.sent_in = f32[2,8,128]{2,1,0:T(8,128)S(1)} collective-permute-done((f32[2,8,128]{2,1,0:T(8,128)S(1)}, f32[2,8,128]{2,1,0:T(8,128)S(1)}, u32[]{:S(2)}, u32[]{:S(2)}) %collective-permute-start.1) | collective-permute-done | bytes 8224 | tf_op jit(solution)/shard_map/ppermute | solution.py:350
  13.6 0.6 %shard_map.107 = (f32[1,16,1024]{2,1,0:T(8,128)S(1)}, bf16[16,1024]{1,0:T(8,128)(2,1)S(1)}, f32[1,16,512]{2,1,0:T(8,128)S(1)}, f32[1,16,512]{2,1,0:T(8,128)S(1)}) custom-call(f32[1]{0:T(128)S(6)} %copy.13.occupation, f32[18,8,128]{2,1,0:T(8,128)S(1)} %get-tuple-element.14.onsite_in, f32[2,8,128]{2,1,0:T(8,128)S(1)} %get-tuple-element.17.outer_in, ...), custom_call_target="tpu_custom_call" | custom-call | flops 33554432 | bytes 2097152 | tf_op jit(solution)/shard_map/pallas_call | solution.py:376
  14.2 0.0 collective-permute-start.4
  14.2 1.9 %collective-permute-start.3 = (f32[16,512]{1,0:T(8,128)S(1)}, f32[16,512]{1,0:T(8,128)S(1)}, u32[]{:S(2)}, u32[]{:S(2)}) collective-permute-start(f32[16,512]{1,0:T(8,128)S(1)} %bitcast.6), channel_id=1, source_target_pairs={{0,2},{1,3},{2,0},{3,1},{4,6},{5,7},{6,4},{7,5},{8,10},{9,11},{10,... | collective-permute-start | bytes 98312 | tf_op jit(solution)/shard_map/ppermute | solution.py:408
  16.0 0.2 %shard_map.109 = f32[1,16,512]{2,1,0:T(8,128)S(1)} custom-call(bf16[16,1024]{1,0:T(8,128)(2,1)S(1)} %get-tuple-element.20.half, bf16[1,1024,2048]{2,1,0:T(8,128)(2,1)S(1)} %copy-done, f32[1,16,512]{2,1,0:T(8,128)S(1)} %get-tuple-element.22.after.rest_0_), custom_call_target="tpu_custom_call" | custom-call | flops 32768 | bytes 2048 | tf_op jit(solution)/shard_map/pallas_call | solution.py:391
  16.3 0.1 collective-permute-start.2
  16.4 0.6 %shard_map.108 = (f32[1,16,512]{2,1,0:T(8,128)S(1)}, f32[1,16,1024]{2,1,0:T(8,128)}) custom-call(bf16[16,1024]{1,0:T(8,128)(2,1)S(1)} %get-tuple-element.20.half, bf16[1,1024,2048]{2,1,0:T(8,128)(2,1)S(1)} %copy-done, f32[1,16,1024]{2,1,0:T(8,128)S(1)} %get-tuple-element.21.charge, f32[1,16,512]{2,1,0:T(8,128)S(1)} %get-tuple-element.22.after.rest_0_), custom_call_target="tpu_custom_call" | custom-call | flops 32768 | bytes 2048 | tf_op jit(solution)/shard_map/pallas_call | solution.py:419
  17.0 0.5 %collective-permute-done.4 = f32[16,512]{1,0:T(8,128)S(1)} collective-permute-done((f32[16,512]{1,0:T(8,128)S(1)}, f32[16,512]{1,0:T(8,128)S(1)}, u32[]{:S(2)}, u32[]{:S(2)}) %collective-permute-start.4) | collective-permute-done | bytes 32800 | tf_op jit(solution)/shard_map/ppermute | solution.py:408
  17.5 0.7 %collective-permute-done.3 = f32[16,512]{1,0:T(8,128)S(1)} collective-permute-done((f32[16,512]{1,0:T(8,128)S(1)}, f32[16,512]{1,0:T(8,128)S(1)}, u32[]{:S(2)}, u32[]{:S(2)}) %collective-permute-start.3) | collective-permute-done | bytes 32800 | tf_op jit(solution)/shard_map/ppermute | solution.py:408
  18.2 0.0 collective-permute-done.2
  18.2 0.6 %fusion = f32[16,512]{1,0:T(8,128)} fusion(f32[16,512]{1,0:T(8,128)S(1)} %collective-permute-done.4, f32[16,512]{1,0:T(8,128)S(1)} %collective-permute-done.3, f32[1,16,512]{2,1,0:T(8,128)S(1)} %get-tuple-element.24, f32[1,16,512]{2,1,0:T(8,128)S(1)} %collective-permute-done.2), kind=kLoop, calls=%fused_computation.1 | loop fusion | flops 24576 | bytes 163840 | tf_op jit(solution)/shard_map/add | solution.py:432
  (2 shorter events, 0.0 us)
Async XLA Ops:
  0.6 2.0 %copy-start.1 = (bf16[16,2048]{1,0:T(8,128)(2,1)S(1)}, bf16[16,2048]{1,0:T(8,128)(2,1)}, u32[]{:S(2)}) copy-start(bf16[16,2048]{1,0:T(8,128)(2,1)} %potential.1) | copy-start | bytes 196612
  0.6 2.0 %copy-start.4 = (f32[1,1024]{1,0:T(1,128)S(1)}, f32[1,1024]{1,0:T(1,128)}, u32[]{:S(2)}) copy-start(f32[1,1024]{1,0:T(1,128)} %mode_energy.1) | copy-start | bytes 12292
  0.7 2.0 %copy-start.5 = (f32[1,1024]{1,0:T(1,128)S(1)}, f32[1,1024]{1,0:T(1,128)}, u32[]{:S(2)}) copy-start(f32[1,1024]{1,0:T(1,128)} %broadening.1) | copy-start | bytes 12292
  0.7 2.0 %copy-start.2 = (f32[1,2,1024]{2,1,0:T(2,128)S(1)}, f32[1,2,1024]{2,1,0:T(2,128)}, u32[]{:S(2)}) copy-start(f32[1,2,1024]{2,1,0:T(2,128)} %self_left.1) | copy-start | bytes 24580
  0.7 2.0 %copy-start.3 = (f32[1,2,1024]{2,1,0:T(2,128)S(1)}, f32[1,2,1024]{2,1,0:T(2,128)}, u32[]{:S(2)}) copy-start(f32[1,2,1024]{2,1,0:T(2,128)} %self_right.1) | copy-start | bytes 24580
  0.7 2.3 %copy-start = (bf16[1,1024,2048]{2,1,0:T(8,128)(2,1)S(1)}, bf16[1,1024,2048]{2,1,0:T(8,128)(2,1)}, u32[]{:S(2)}) copy-start(bf16[1,1024,2048]{2,1,0:T(8,128)(2,1)} %profile.7) | copy-start | bytes 12582916
  3.9 4.9 %collective-permute-start = (f32[6,8,128]{2,1,0:T(8,128)S(1)}, f32[6,8,128]{2,1,0:T(8,128)S(1)}, u32[]{:S(2)}, u32[]{:S(2)}) collective-permute-start(f32[6,8,128]{2,1,0:T(8,128)S(1)} %get-tuple-element.16.refs_1_), channel_id=1, source_target_pairs={{0,4},{4,0},{8,12},{12,8},{1,5},{5,1},{9,13},{13,9},{2,6},{6,2},{1... | collective-permute-start | bytes 73736 | tf_op jit(solution)/shard_map/ppermute | solution.py:339
  8.9 4.7 %collective-permute-start.1 = (f32[2,8,128]{2,1,0:T(8,128)S(1)}, f32[2,8,128]{2,1,0:T(8,128)S(1)}, u32[]{:S(2)}, u32[]{:S(2)}) collective-permute-start(f32[2,8,128]{2,1,0:T(8,128)S(1)} %get-tuple-element.19), channel_id=1, source_target_pairs={{0,8},{4,12},{8,0},{12,4},{1,9},{5,13},{9,1},{13,5},{2,10},{6,14},... | collective-permute-start | bytes 24584 | tf_op jit(solution)/shard_map/ppermute | solution.py:350
  14.2 3.4 %collective-permute-start.4 = (f32[16,512]{1,0:T(8,128)S(1)}, f32[16,512]{1,0:T(8,128)S(1)}, u32[]{:S(2)}, u32[]{:S(2)}) collective-permute-start(f32[16,512]{1,0:T(8,128)S(1)} %bitcast.7), channel_id=1, source_target_pairs={{0,3},{1,2},{2,1},{3,0},{4,7},{5,6},{6,5},{7,4},{8,11},{9,10},{10,... | collective-permute-start | bytes 98312 | tf_op jit(solution)/shard_map/ppermute | solution.py:408
  14.2 4.1 %collective-permute-start.3 = (f32[16,512]{1,0:T(8,128)S(1)}, f32[16,512]{1,0:T(8,128)S(1)}, u32[]{:S(2)}, u32[]{:S(2)}) collective-permute-start(f32[16,512]{1,0:T(8,128)S(1)} %bitcast.6), channel_id=1, source_target_pairs={{0,2},{1,3},{2,0},{3,1},{4,6},{5,7},{6,4},{7,5},{8,10},{9,11},{10,... | collective-permute-start | bytes 98312 | tf_op jit(solution)/shard_map/ppermute | solution.py:408
  16.3 2.0 %collective-permute-start.2 = (f32[1,16,512]{2,1,0:T(8,128)S(1)}, f32[1,16,512]{2,1,0:T(8,128)S(1)}, u32[]{:S(2)}, u32[]{:S(2)}) collective-permute-start(f32[1,16,512]{2,1,0:T(8,128)S(1)} %shard_map.109), channel_id=1, source_target_pairs={{0,1},{1,0},{2,3},{3,2},{4,5},{5,4},{6,7},{7,6},{8,9},{9,8},{10,11... | collective-permute-start | bytes 98312 | tf_op jit(solution)/shard_map/ppermute | solution.py:370
